TPU v7x, 256 devices: a whole 4x4x8 slice. The times are simulated.
256 devices in a mesh: dp: 32 (over x, y, core), tensor: 8 (over z).
Axes of the slice: x: 4, y: 4, z: 8, core: 2. Of those that a mesh axis runs over, the one named last changes fastest.
Arguments:
- activations: bfloat16 [24576, 16384], P('dp', 'tensor'), may hold values from -6 to 6
- cotangent: bfloat16 [24576, 2048], P('dp', 'tensor'), may hold values from -0.59765625 to 0.59765625
- master: float32 [16384, 2048], P('dp', 'tensor')
- moment_one: float32 [16384, 2048], P('dp', 'tensor'), may hold values from -6 to 6
- moment_two: float32 [16384, 2048], P('dp', 'tensor'), may hold values from 0.25 to 4
- writer_of: int32 [16384], replicated, may hold values from 0 to 31, as said below
- previous: float32 [32768, 2048], P('dp', 'tensor'), as said below
Outputs:
- checkpoint_delta: float32 [32768, 2048], P('dp', 'tensor')
- delta_high: bfloat16 [32768, 2048], P('dp', 'tensor')
- moment_one_out: float32 [32768, 2048], P('dp', 'tensor')
- moment_two_out: float32 [32768, 2048], P('dp', 'tensor')
Inputs may be any that keep to these rules, and one draw needn't show every extreme that they name: `writer_of`: within each aligned block of 512 rows (the rows of one owner) no writer is named more than 32 times, so no writer is named by more than 1024 rows; in every draw one writer is named exactly 32 times in every block and so by exactly 1024 rows. Rows of previous that some slot names lie within 0.3 of the master row that goes there.
All inputs are finite; a program needn't handle non-finite values.
Results may differ from a plain program's by a relative error of at most 0.001.
Values may be sent and summed in bfloat16 or wider, within the bound.
A program may use at most 128 MiB of HBM per device.

v0:
```python
import jax
import jax.numpy as jnp
from jax import lax
from jax.sharding import PartitionSpec as P

learn_rate = 0.01
beta_one = 0.9
beta_two = 0.95
epsilon = 1e-08
decay_rate = 0.1
bias_one = 1.0 - 0.9**10
bias_two = 1.0 - 0.95**10


def adam_rows(gradient, master, moment_one, moment_two):
    first = beta_one * moment_one + (1.0 - beta_one) * gradient
    second = beta_two * moment_two + (1.0 - beta_two) * gradient * gradient
    step_dir = first / bias_one / (jnp.sqrt(second / bias_two) + epsilon) + decay_rate * master
    return (master - learn_rate * step_dir, first, second)


def local(activations, cotangent, master, moment_one, moment_two, writer_of, previous):
    owner_count = lax.axis_size("dp")
    owner_index = lax.axis_index("dp")
    row_dev = master.shape[0]
    capacity = previous.shape[0]
    pair_slots = capacity // owner_count
    gathered = lax.all_gather(activations, "tensor", axis=1, tiled=True)
    writer_ids = jnp.arange(owner_count, dtype=jnp.int32)
    owner_onehot = (
        writer_of.reshape(owner_count, row_dev)[:, :, None] == writer_ids[None, None, :]
    ).astype(jnp.int32)
    counts = jnp.sum(owner_onehot, axis=1)
    base_slot = jnp.cumsum(counts, axis=0) - counts
    local_onehot = lax.dynamic_index_in_dim(owner_onehot, owner_index, 0, keepdims=False)
    local_writers = lax.dynamic_slice_in_dim(writer_of, owner_index * row_dev, row_dev, 0)
    local_rank = jnp.sum((jnp.cumsum(local_onehot, axis=0) - local_onehot) * local_onehot, axis=1)
    source_base = lax.dynamic_slice_in_dim(base_slot, owner_index, 1, 1)[:, 0]
    source_count = lax.dynamic_slice_in_dim(counts, owner_index, 1, 1)[:, 0]
    slot_ids = jnp.arange(pair_slots, dtype=jnp.int32)
    target = jnp.where(
        slot_ids[None, :] < source_count[:, None],
        source_base[:, None] + slot_ids[None, :],
        capacity,
    ).reshape(-1)
    filled = jnp.arange(capacity, dtype=jnp.int32) < jnp.sum(source_count)

    def pack_rows(values):
        buffer = jnp.zeros((owner_count, pair_slots, values.shape[1]), jnp.float32)
        return buffer.at[local_writers, local_rank].set(values)

    def unpack_rows(received):
        width = received.shape[2]
        flat = received.reshape(owner_count * pair_slots, width)
        return jnp.zeros((capacity, width), jnp.float32).at[target].set(flat, mode="drop")

    gradient = lax.psum_scatter(
        jnp.einsum("tr,tc->rc", gathered, cotangent, preferred_element_type=jnp.float32),
        "dp",
        scatter_dimension=0,
        tiled=True,
    )
    updated, first, second = adam_rows(gradient, master, moment_one, moment_two)
    received = (
        lax.all_to_all(pack_rows(updated), "dp", split_axis=0, concat_axis=0, tiled=True),
        lax.all_to_all(pack_rows(first), "dp", split_axis=0, concat_axis=0, tiled=True),
        lax.all_to_all(pack_rows(second), "dp", split_axis=0, concat_axis=0, tiled=True),
    )
    updated_slots = unpack_rows(received[0])
    first_slots = unpack_rows(received[1])
    second_slots = unpack_rows(received[2])
    delta_out = jnp.where(filled[:, None], (updated_slots - previous) / learn_rate, 0.0)
    delta_out, first_out, second_out = (delta_out, first_slots, second_slots)
    return (delta_out, delta_out.astype(jnp.bfloat16), first_out, second_out)


def solution(mesh):
    in_specs = (
        P("dp", "tensor"),
        P("dp", "tensor"),
        P("dp", "tensor"),
        P("dp", "tensor"),
        P("dp", "tensor"),
        P(),
        P("dp", "tensor"),
    )
    out_specs = (P("dp", "tensor"), P("dp", "tensor"), P("dp", "tensor"), P("dp", "tensor"))
    return jax.shard_map(local, mesh=mesh, in_specs=in_specs, out_specs=out_specs, check_vma=False)
```

profile of v0, /device:TPU:57, one launch (start us, length us, event | category | flops | bytes accessed | tf_op | source)
XLA Modules:
  0.0 626.1 jit_solution(3995231380278099528)
XLA Ops:
  7.2 0.7 all-gather.2.cloned.1.call-update
  8.0 253.9 %all-gather.2.cloned.1.call-done = bf16[768,16384]{1,0:T(8,128)(2,1)} async-done(((bf16[768,2048]{1,0:T(8,128)(2,1)}), bf16[768,16384]{1,0:T(8,128)(2,1)}) %all-gather.2.cloned.1.call-update) | async-done | bytes 25165840 | tf_op jit(solution)/shard_map/all_gather | solution.py:28
  261.8 14.9 %fusion.14 = f32[16384,256]{1,0:T(8,128)} fusion(bf16[768,16384]{1,0:T(8,128)(2,1)} %all-gather.2.cloned.1.call-done, bf16[768,256]{1,0:T(8,128)(2,1)S(1)} %copy-done), kind=kOutput, calls=%fused_computation.42 | convolution fusion | flops 6442450944 | bytes 42336256 | tf_op jit(solution)/shard_map/tr,tc->rc/dot_general | solution.py:58
  276.7 0.8 copy-done.5
  277.8 1.2 reduce-window.6
  279.5 119.2 %reduce-scatter.2.cloned.1.call-done = f32[512,256]{1,0:T(8,128)} async-done(((f32[16384,256]{1,0:T(8,128)}), f32[512,256]{1,0:T(8,128)}) %reduce-scatter.2.cloned.1.call-update) | async-done | bytes 524304 | tf_op jit(solution)/shard_map/reduce_scatter | solution.py:57
  398.7 1.8 multiply_subtract_fusion
  400.5 1.1 broadcast.78.clone
  401.6 56.7 %scatter_fusion = f32[32,32,256]{2,1,0:T(8,128)} fusion(f32[32,32,256]{2,1,0:T(8,128)} %broadcast.78.clone, s32[512]{0:T(512)S(1)} %bitcast.35, f32[512,256]{1,0:T(8,128)S(1)} %get-tuple-element.9), kind=kCustom, calls=%fused_computation | custom fusion | bytes 1576960 | tf_op jit(solution)/shard_map/scatter | solution.py:50
  458.3 7.2 %all-to-all-start = ((f32[32,32,256]{2,1,0:T(8,128)}), f32[32,32,256]{2,1,0:T(8,128)S(1)}, u32[]{:S(2)}, u32[]{:S(2)}) async-start(f32[32,32,256]{2,1,0:T(8,128)} %scatter_fusion), calls=%async_computation.1 | async-start | bytes 2097152 | tf_op jit(solution)/shard_map/all_to_all | solution.py:65
  465.5 1.1 broadcast.78.clone.1
  466.6 56.7 %scatter_fusion.1 = f32[32,32,256]{2,1,0:T(8,128)} fusion(f32[32,32,256]{2,1,0:T(8,128)} %broadcast.78.clone.1, s32[512]{0:T(512)S(1)} %bitcast.36, f32[512,256]{1,0:T(8,128)S(1)} %get-tuple-element.10), kind=kCustom, calls=%fused_computation.2 | custom fusion | bytes 1576960 | tf_op jit(solution)/shard_map/scatter | solution.py:50
  523.3 7.3 %all-to-all-start.1 = ((f32[32,32,256]{2,1,0:T(8,128)}), f32[32,32,256]{2,1,0:T(8,128)S(1)}, u32[]{:S(2)}, u32[]{:S(2)}) async-start(f32[32,32,256]{2,1,0:T(8,128)} %scatter_fusion.1), calls=%async_computation.2 | async-start | bytes 2097152 | tf_op jit(solution)/shard_map/all_to_all | solution.py:66
  530.7 1.1 broadcast.78.clone.2
  531.8 56.7 %scatter_fusion.2 = f32[32,32,256]{2,1,0:T(8,128)} fusion(f32[32,32,256]{2,1,0:T(8,128)} %broadcast.78.clone.2, s32[512]{0:T(512)S(1)} %bitcast.37, f32[512,256]{1,0:T(8,128)S(1)} %get-tuple-element.11), kind=kCustom, calls=%fused_computation.4 | custom fusion | bytes 1576960 | tf_op jit(solution)/shard_map/scatter | solution.py:50
  588.5 7.5 %all-to-all-start.2 = ((f32[32,32,256]{2,1,0:T(8,128)}), f32[32,32,256]{2,1,0:T(8,128)}, u32[]{:S(2)}, u32[]{:S(2)}) async-start(f32[32,32,256]{2,1,0:T(8,128)} %scatter_fusion.2), calls=%async_computation.3 | async-start | bytes 2097152 | tf_op jit(solution)/shard_map/all_to_all | solution.py:67
  596.0 0.6 fusion.1
  596.7 0.7 dynamic-slice_reduce_fusion.1
  597.6 0.7 iota_compare_fusion.2
  598.3 5.2 scatter_custom_fusion.1
  603.5 5.8 scatter_custom_fusion.3
  609.3 2.3 all-to-all-done.2
  611.6 6.3 scatter_custom_fusion.5
  617.9 1.4 fusion.12
  (29 shorter events, 1.1 us)
Async XLA Ops:
  7.2 254.7 %copy-start = (bf16[768,256]{1,0:T(8,128)(2,1)S(1)}, bf16[768,256]{1,0:T(8,128)(2,1)}, u32[]{:S(2)}) copy-start(bf16[768,256]{1,0:T(8,128)(2,1)} %param.8) | copy-start | bytes 1179652
  7.2 254.7 %all-gather.2.cloned.1.call-start = ((), (), s32[]{:S(2)}) async-start(), calls=%async_computation.4 | async-start | bytes 28311552 | tf_op jit(solution)/shard_map/all_gather | solution.py:28
  7.9 390.8 %reduce-scatter.2.cloned.1.call-start = ((), (), s32[]{:S(2)}) async-start(), calls=%async_computation.5 | async-start | bytes 17301504 | tf_op jit(solution)/shard_map/reduce_scatter | solution.py:57
  276.7 0.8 copy-start.5
  276.7 122.0 %copy-start.4 = (f32[512,256]{1,0:T(8,128)S(1)}, f32[512,256]{1,0:T(8,128)}, u32[]{:S(2)}) copy-start(f32[512,256]{1,0:T(8,128)} %param.9) | copy-start | bytes 1572868
  277.5 122.9 %copy-start.2 = (s32[32,512]{1,0:T(8,128)}, s32[32,512]{1,0:T(8,128)S(1)}, u32[]{:S(2)}) copy-start(s32[32,512]{1,0:T(8,128)S(1)} %eq.15) | copy-start | bytes 196612
  458.3 65.0 %all-to-all-start = ((f32[32,32,256]{2,1,0:T(8,128)}), f32[32,32,256]{2,1,0:T(8,128)S(1)}, u32[]{:S(2)}, u32[]{:S(2)}) async-start(f32[32,32,256]{2,1,0:T(8,128)} %scatter_fusion), calls=%async_computation.1 | async-start | bytes 2097152 | tf_op jit(solution)/shard_map/all_to_all | solution.py:65
  523.3 65.2 %all-to-all-start.1 = ((f32[32,32,256]{2,1,0:T(8,128)}), f32[32,32,256]{2,1,0:T(8,128)S(1)}, u32[]{:S(2)}, u32[]{:S(2)}) async-start(f32[32,32,256]{2,1,0:T(8,128)} %scatter_fusion.1), calls=%async_computation.2 | async-start | bytes 2097152 | tf_op jit(solution)/shard_map/all_to_all | solution.py:66
  588.5 7.5 %copy-start.3 = (s32[32,512]{1,0:T(8,128)S(1)}, s32[32,512]{1,0:T(8,128)}, u32[]{:S(2)}) copy-start(s32[32,512]{1,0:T(8,128)} %copy-done.2) | copy-start | bytes 196612
  588.5 23.1 %all-to-all-start.2 = ((f32[32,32,256]{2,1,0:T(8,128)}), f32[32,32,256]{2,1,0:T(8,128)}, u32[]{:S(2)}, u32[]{:S(2)}) async-start(f32[32,32,256]{2,1,0:T(8,128)} %scatter_fusion.2), calls=%async_computation.3 | async-start | bytes 2097152 | tf_op jit(solution)/shard_map/all_to_all | solution.py:67
  603.5 14.3 %copy-start.1 = (f32[1024,256]{1,0:T(8,128)S(1)}, f32[1024,256]{1,0:T(8,128)}, u32[]{:S(2)}) copy-start(f32[1024,256]{1,0:T(8,128)} %param.13) | copy-start | bytes 3145732
Sparse Core Ops, SparseCore 0:
  9.8 251.9 all-gather.1
  276.8 121.8 reduce-scatter.1
where the time goes:
time: 635 us; the launch traced here: 626 us
  waiting for transfers between devices  376 us (59%)
  local copies, waits for them, and re-layouts  192 us (30%)
  starting transfers between devices  22.2 us (3%)
  matrix products  14.9 us (2%)
  between operations  14.2 us (2%)
  other arithmetic  6.92 us (1%)
    all_gather x1, waiting for transfers between devices, local(): gathered = lax.all_gather(activations, 'tensor', axis=1, tiled=True)  254 us
    scatter x3, local copies, waits for them, and re-layouts, pack_rows(): return buffer.at[local_writers, local_rank].set(values)  170 us
    reduce_scatter x1, waiting for transfers between devices, local(): lax.psum_scatter(jnp.einsum('tr,tc->rc', gathered, cotangent, preferred_e...  119 us
    scatter x3, local copies, waits for them, and re-layouts, unpack_rows(): jnp.zeros((capacity, width), jnp.float32).at[target].set(flat, mode='drop')  17.3 us
    dot_general x1, matrix products, local(): jnp.einsum('tr,tc->rc', gathered, cotangent, preferred_element_type=jnp.f...  14.9 us
  transfers between devices with their start and end apart: 5, of which 3 were waited for; matrix products, arithmetic and copies ran while one was open for 21% of the time, Pallas kernels for 0%

commit v1 on v0

v1 whole, which is shorter than its diff:
```python
import functools

import jax
import jax.numpy as jnp
from jax import lax
from jax.experimental import pallas as pl
from jax.experimental.pallas import tpu as pltpu
from jax.sharding import PartitionSpec as P

learn_rate = 0.01
beta_one = 0.9
beta_two = 0.95
epsilon = 1e-08
decay_rate = 0.1
bias_one = 1.0 - 0.9**10
bias_two = 1.0 - 0.95**10


def adam_rows(gradient, master, moment_one, moment_two):
    first = beta_one * moment_one + (1.0 - beta_one) * gradient
    second = beta_two * moment_two + (1.0 - beta_two) * gradient * gradient
    step_dir = first / bias_one / (jnp.sqrt(second / bias_two) + epsilon) + decay_rate * master
    return (master - learn_rate * step_dir, first, second)


def unpack_kernel(base_ref, received_ref, previous_ref, delta_ref, high_ref, first_ref, second_ref, rows_ref):
    sources, pair, _ = received_ref.shape
    capacity, width = previous_ref.shape
    window = pair + 8
    row = lax.broadcasted_iota(jnp.int32, (window, 3 * width), 0)
    for source in range(sources):
        start = base_ref[source]
        shift = lax.rem(start, 8)
        aligned = pl.multiple_of(start - shift, 8)
        block = jnp.concatenate([received_ref[source], received_ref[source, 0:8]], axis=0)
        block = pltpu.roll(block, shift, 0)
        target = rows_ref.at[pl.ds(aligned, window), :]
        target[...] = jnp.where(row >= shift, block, target[...])
    filled = lax.broadcasted_iota(jnp.int32, (capacity, width), 0) < base_ref[sources]
    delta = jnp.where(filled, (rows_ref[0:capacity, 0:width] - previous_ref[...]) / learn_rate, 0.0)
    delta_ref[...] = delta
    high_ref[...] = delta.astype(jnp.bfloat16)
    first_ref[...] = jnp.where(filled, rows_ref[0:capacity, width : 2 * width], 0.0)
    second_ref[...] = jnp.where(filled, rows_ref[0:capacity, 2 * width : 3 * width], 0.0)


def unpack(base, received, previous):
    capacity, width = previous.shape
    pair = received.shape[1]
    vmem = pl.BlockSpec(memory_space=pltpu.VMEM)
    return pl.pallas_call(
        unpack_kernel,
        out_shape=(
            jax.ShapeDtypeStruct((capacity, width), jnp.float32),
            jax.ShapeDtypeStruct((capacity, width), jnp.bfloat16),
            jax.ShapeDtypeStruct((capacity, width), jnp.float32),
            jax.ShapeDtypeStruct((capacity, width), jnp.float32),
        ),
        in_specs=[pl.BlockSpec(memory_space=pltpu.SMEM), vmem, vmem],
        out_specs=(vmem, vmem, vmem, vmem),
        scratch_shapes=[pltpu.VMEM((capacity + pair + 8, received.shape[2]), jnp.float32)],
        compiler_params=pltpu.CompilerParams(vmem_limit_bytes=48 * 1024 * 1024),
    )(base, received, previous)


def local(activations, cotangent, master, moment_one, moment_two, writer_of, previous):
    owners = lax.axis_size("dp")
    planes = lax.axis_size("tensor")
    index = lax.axis_index("dp")
    row_dev, width = master.shape
    capacity = previous.shape[0]
    pair = capacity // owners
    local_owners = owners // planes

    columns = lax.all_gather(cotangent, "tensor", axis=0)
    partial = jnp.einsum(
        "tor,ctk->ocrk",
        activations.reshape(-1, local_owners, row_dev),
        columns,
        preferred_element_type=jnp.float32,
    )
    piece = lax.psum_scatter(
        partial.reshape(owners * row_dev, width), "dp", scatter_dimension=0, tiled=True
    )
    perm = []
    for i in range(owners):
        for t in range(planes):
            perm.append((i * planes + t, (local_owners * t + i // planes) * planes + i % planes))
    gradient = lax.ppermute(piece, ("dp", "tensor"), perm)

    onehot = (
        writer_of.reshape(owners, row_dev)[:, :, None] == jnp.arange(owners, dtype=jnp.int32)
    ).astype(jnp.float32)
    counts = jnp.sum(onehot, axis=1)
    totals = jnp.cumsum(counts, axis=0)
    base = lax.dynamic_slice_in_dim(totals - counts, index, 1, 1)[:, 0]
    total = lax.dynamic_slice_in_dim(totals[-1], index, 1, 0)
    base = jnp.concatenate([base, total]).astype(jnp.int32)

    mine = lax.dynamic_index_in_dim(onehot, index, 0, keepdims=False)
    below = jnp.tril(jnp.ones((row_dev, row_dev), jnp.float32), -1)
    rank = jnp.sum(jnp.dot(below, mine) * mine, axis=1).astype(jnp.int32)
    local_writers = lax.dynamic_slice_in_dim(writer_of, index * row_dev, row_dev, 0)
    place = local_writers * pair + rank
    pack = (jnp.arange(capacity, dtype=jnp.int32)[:, None] == place[None, :]).astype(jnp.float32)

    rows = jnp.concatenate(adam_rows(gradient, master, moment_one, moment_two), axis=1)
    packed = jnp.dot(pack, rows, precision=lax.Precision.HIGHEST)
    received = lax.all_to_all(
        packed.reshape(owners, pair, 3 * width), "dp", split_axis=0, concat_axis=0, tiled=True
    )
    return unpack(base, received, previous)


def solution(mesh):
    spec = P("dp", "tensor")
    return jax.shard_map(
        local,
        mesh=mesh,
        in_specs=(spec, spec, spec, spec, spec, P(), spec),
        out_specs=(spec, spec, spec, spec),
        check_vma=False,
    )
```

time: 635 us -> 327 us (0.51)
  local copies, waits for them, and re-layouts: 192 us -> 19 us
  waiting for transfers between devices: 376 us -> 229 us
  starting transfers between devices: 22.2 us -> 33.7 us
    all_gather x1, waiting for transfers between devices: 254 us -> 47.6 us  [local(): columns = lax.all_gather(cotangent, 'tensor', axis=0)]
    scatter x6 -> x0, local copies, waits for them, and re-layouts: 187 us -> none  [the longest x3 170 us: pack_rows(): return buffer.at[local_writers, local_rank].set(values)]
    all_to_all x3 -> x1, waiting for transfers between devices: 2.29 us -> 36.6 us  [local(): lax.all_to_all(packed.reshape(owners, pair, 3 * width), 'dp', split_axis=...]
    ppermute x0 -> x1, waiting for transfers between devices: none -> 23.6 us  [local(): gradient = lax.ppermute(piece, ('dp', 'tensor'), perm)]
    transpose x0 -> x1, local copies, waits for them, and re-layouts: none -> 16.4 us  [local(): jnp.einsum('tor,ctk->ocrk', activations.reshape(-1, local_owners, row_dev...]
    ppermute x0 -> x1, starting transfers between devices: none -> 6.68 us  [local(): gradient = lax.ppermute(piece, ('dp', 'tensor'), perm)]
    all_to_all x3 -> x1, starting transfers between devices: 22.1 us -> 26.9 us  [local(): lax.all_to_all(packed.reshape(owners, pair, 3 * width), 'dp', split_axis=...]
    dot_general x1 -> x3, matrix products: 14.9 us -> 18.4 us  [the longest x1 12.7 us: local(): jnp.einsum('tor,ctk->ocrk', activations.reshape(-1, local_owners, row_dev...]
  transfers between devices with their start and end apart: 5 -> 4, of which waited for: 3 -> 4; matrix products, arithmetic and copies ran while one was open for 21% -> 1% of each run, Pallas kernels for 0% -> 0%
where the time goes in v1:
time: 327 us; the launch traced here: 322 us
  waiting for transfers between devices  229 us (70%)
  starting transfers between devices  33.7 us (10%)
  local copies, waits for them, and re-layouts  19 us (6%)
  matrix products  18.4 us (6%)
  between operations  14.1 us (4%)
  other arithmetic  4.32 us (1%)
  Pallas kernels  3.56 us (1%)
    reduce_scatter x1, waiting for transfers between devices, local(): lax.psum_scatter(partial.reshape(owners * row_dev, width), 'dp', scatter_...  121 us
    all_gather x1, waiting for transfers between devices, local(): columns = lax.all_gather(cotangent, 'tensor', axis=0)  47.6 us
    all_to_all x1, waiting for transfers between devices, local(): lax.all_to_all(packed.reshape(owners, pair, 3 * width), 'dp', split_axis=...  36.6 us
    all_to_all x1, starting transfers between devices, local(): lax.all_to_all(packed.reshape(owners, pair, 3 * width), 'dp', split_axis=...  26.9 us
    ppermute x1, waiting for transfers between devices, local(): gradient = lax.ppermute(piece, ('dp', 'tensor'), perm)  23.6 us
    transpose x1, local copies, waits for them, and re-layouts, local(): jnp.einsum('tor,ctk->ocrk', activations.reshape(-1, local_owners, row_dev...  16.4 us
    dot_general x1, matrix products, local(): jnp.einsum('tor,ctk->ocrk', activations.reshape(-1, local_owners, row_dev...  12.7 us
    ppermute x1, starting transfers between devices, local(): gradient = lax.ppermute(piece, ('dp', 'tensor'), perm)  6.68 us
  transfers between devices with their start and end apart: 4, of which 4 were waited for; matrix products, arithmetic and copies ran while one was open for 1% of the time, Pallas kernels for 0%

profile of v1, /device:TPU:57, one launch (start us, length us, event | category | flops | bytes accessed | tf_op | source)
XLA Modules:
  0.0 322.4 jit_solution(187543068723510151)
XLA Ops:
  7.2 0.0 all-gather.3.cloned.1.call-start
  7.2 0.7 all-gather.3.cloned.1.call-update
  7.9 0.0 reduce-scatter.2.cloned.1.call-start
  7.9 47.6 %all-gather.3.cloned.1.call-done = bf16[6144,256]{1,0:T(8,128)(2,1)} async-done(((bf16[768,256]{1,0:T(8,128)(2,1)}), bf16[6144,256]{1,0:T(8,128)(2,1)}) %all-gather.3.cloned.1.call-update) | async-done | bytes 3145744 | tf_op jit(solution)/shard_map/all_gather | solution.py:75
  55.5 12.7 %convolution_bitcast_fusion = f32[4,8,512,256]{2,3,0,1:T(8,128)} fusion(bf16[8,768,256,1]{2,1,3,0:T(8,128)(2,1)} %bitcast.26, bf16[96,4,8,512]{3,2,1,0:T(8,128)(2,1)} %bitcast.25), kind=kOutput, calls=%fused_computation | convolution fusion | flops 6442450944 | bytes 23068672 | tf_op jit(solution)/shard_map/tor,ctk->ocrk/dot_general | solution.py:76
  68.2 16.4 %copy.17 = f32[4,8,512,256]{3,2,1,0:T(8,128)} copy(f32[4,8,512,256]{2,3,0,1:T(8,128)} %convolution_bitcast_fusion) | data formatting | bytes 33554432 | tf_op jit(solution)/shard_map/tor,ctk->ocrk/transpose | solution.py:76
  84.6 0.8 copy-done.3
  85.5 120.9 %reduce-scatter.2.cloned.1.call-done = f32[512,256]{1,0:T(8,128)} async-done(((f32[16384,256]{1,0:T(8,128)}), f32[512,256]{1,0:T(8,128)}) %reduce-scatter.2.cloned.1.call-update) | async-done | bytes 524304 | tf_op jit(solution)/shard_map/reduce_scatter | solution.py:82
  206.4 6.7 %collective-permute-start = (f32[512,256]{1,0:T(8,128)}, f32[512,256]{1,0:T(8,128)}, u32[]{:S(2)}, u32[]{:S(2)}) collective-permute-start(f32[512,256]{1,0:T(8,128)} %reduce-scatter.2.cloned.1.call-done), channel_id=1, source_target_pairs={{0,0},{1,32},{2,64},{3,96},{4,128},{5,160},{6,192},{7,224},{8,1},{... | collective-permute-start | bytes 1572872 | tf_op jit(solution)/shard_map/ppermute | solution.py:89
  213.1 1.4 iota_compare_fusion.1
  214.4 1.1 fusion.7
  215.5 0.1 convert_add_fusion
  215.6 23.6 %collective-permute-done = f32[512,256]{1,0:T(8,128)} collective-permute-done((f32[512,256]{1,0:T(8,128)}, f32[512,256]{1,0:T(8,128)}, u32[]{:S(2)}, u32[]{:S(2)}) %collective-permute-start) | collective-permute-done | bytes 524320 | tf_op jit(solution)/shard_map/ppermute | solution.py:89
  239.2 1.6 multiply_subtract_fusion
  240.8 4.6 %fusion.1 = f32[1024,768]{1,0:T(8,128)} fusion(f32[512,256]{1,0:T(8,128)S(1)} %get-tuple-element.6, f32[512,256]{1,0:T(8,128)S(1)} %get-tuple-element.5, f32[512,256]{1,0:T(8,128)S(1)} %get-tuple-element.4, s32[512]{0:T(512)S(1)} %convert_add_fusion), kind=kOutput, calls=%fused_computation.5 | convolution fusion | flops 4833148928 | bytes 4720640 | tf_op jit(solution)/shard_map/dot_general | solution.py:108
  245.4 26.9 %all-to-all-start = ((f32[32,32,768]{2,1,0:T(8,128)}), f32[32,32,768]{2,1,0:T(8,128)S(1)}, u32[]{:S(2)}, u32[]{:S(2)}) async-start(f32[32,32,768]{2,1,0:T(8,128)} %bitcast.24), calls=%async_computation.1 | async-start | bytes 6291456 | tf_op jit(solution)/shard_map/all_to_all | solution.py:109
  272.3 0.3 convert_reduce_fusion
  272.6 0.1 reduce_window_sum.11
  272.7 0.6 constant_dynamic-slice_fusion
  273.3 0.2 fusion.16
  273.5 0.7 maximum_convert_fusion.base_ref
  274.2 36.6 %all-to-all-done.received_ref = f32[32,32,768]{2,1,0:T(8,128)S(1)} async-done(((f32[32,32,768]{2,1,0:T(8,128)}), f32[32,32,768]{2,1,0:T(8,128)S(1)}, u32[]{:S(2)}, u32[]{:S(2)}) %all-to-all-start) | async-done | bytes 3145760 | tf_op jit(solution)/shard_map/all_to_all | solution.py:109
  310.8 1.2 copy-done
  312.0 3.6 %shard_map.102 = (f32[1024,256]{1,0:T(8,128)}, bf16[1024,256]{1,0:T(8,128)(2,1)}, f32[1024,256]{1,0:T(8,128)}, f32[1024,256]{1,0:T(8,128)}) custom-call(s32[33]{0:T(128)S(1)} %maximum_convert_fusion.base_ref, f32[32,32,768]{2,1,0:T(8,128)S(1)} %all-to-all-done.received_ref, f32[1024,256]{1,0:T(8,128)S(1)} %copy-done), custom_call_target="tpu_custom_call" | custom-call | tf_op jit(solution)/shard_map/pallas_call | solution.py:51
  (10 shorter events, 0.0 us)
Async XLA Ops:
  7.2 48.4 %all-gather.3.cloned.1.call-start = ((), (), s32[]{:S(2)}) async-start(), calls=%async_computation.3 | async-start | bytes 3538944 | tf_op jit(solution)/shard_map/all_gather | solution.py:75
  7.9 198.5 %reduce-scatter.2.cloned.1.call-start = ((), (), s32[]{:S(2)}) async-start(), calls=%async_computation.2 | async-start | bytes 17301504 | tf_op jit(solution)/shard_map/reduce_scatter | solution.py:82
  84.6 0.8 copy-start.3
  85.4 153.7 %copy-start.1 = (f32[512,256]{1,0:T(8,128)S(1)}, f32[512,256]{1,0:T(8,128)}, u32[]{:S(2)}) copy-start(f32[512,256]{1,0:T(8,128)} %param.9) | copy-start | bytes 1572868
  85.4 153.7 %copy-start.2 = (f32[512,256]{1,0:T(8,128)S(1)}, f32[512,256]{1,0:T(8,128)}, u32[]{:S(2)}) copy-start(f32[512,256]{1,0:T(8,128)} %param.10) | copy-start | bytes 1572868
  206.4 32.8 %collective-permute-start = (f32[512,256]{1,0:T(8,128)}, f32[512,256]{1,0:T(8,128)}, u32[]{:S(2)}, u32[]{:S(2)}) collective-permute-start(f32[512,256]{1,0:T(8,128)} %reduce-scatter.2.cloned.1.call-done), channel_id=1, source_target_pairs={{0,0},{1,32},{2,64},{3,96},{4,128},{5,160},{6,192},{7,224},{8,1},{... | collective-permute-start | bytes 1572872 | tf_op jit(solution)/shard_map/ppermute | solution.py:89
  245.4 65.4 %all-to-all-start = ((f32[32,32,768]{2,1,0:T(8,128)}), f32[32,32,768]{2,1,0:T(8,128)S(1)}, u32[]{:S(2)}, u32[]{:S(2)}) async-start(f32[32,32,768]{2,1,0:T(8,128)} %bitcast.24), calls=%async_computation.1 | async-start | bytes 6291456 | tf_op jit(solution)/shard_map/all_to_all | solution.py:109
  310.8 1.2 copy-start
Sparse Core Ops, SparseCore 0:
  9.8 45.7 all-gather.2
  84.8 121.5 reduce-scatter.1

commit v2 on v1

v2 whole, which is shorter than its diff:
```python
import functools

import jax
import jax.numpy as jnp
from jax import lax
from jax.experimental import pallas as pl
from jax.experimental.pallas import tpu as pltpu
from jax.sharding import PartitionSpec as P

learn_rate = 0.01
beta_one = 0.9
beta_two = 0.95
epsilon = 1e-08
decay_rate = 0.1
bias_one = 1.0 - 0.9**10
bias_two = 1.0 - 0.95**10

MESH = pl.DeviceIdType.MESH
SIDE = 4
CORES = 2
DP = SIDE * SIDE * CORES
PLANES = 8
CHUNKS = 2
SCALE_ROWS = 8
TOP = 14.99
ORDER = ((1, 7), (2, 6), (3, 5))


def adam_rows(gradient, master, moment_one, moment_two):
    first = beta_one * moment_one + (1.0 - beta_one) * gradient
    second = beta_two * moment_two + (1.0 - beta_two) * gradient * gradient
    step_dir = first / bias_one / (jnp.sqrt(second / bias_two) + epsilon) + decay_rate * master
    return (master - learn_rate * step_dir, first, second)


def exponent_of(values):
    most = jnp.max(jnp.abs(values), axis=0, keepdims=True)
    return jnp.ceil(jnp.log2(jnp.maximum(most, 1e-30)))


def encode(values, exponent):
    return jnp.round(values * jnp.exp2(TOP - exponent)).astype(jnp.int32)


def unit_of(exponent):
    return 1.0 / jnp.exp2(TOP - exponent)


def join(high, low):
    return (high << 16) | (low & 0xFFFF)


def high_of(word):
    return word >> 16


def low_of(word):
    return (word << 16) >> 16


def coordinates():
    index = lax.axis_index("dp")
    return index // (SIDE * CORES), (index // CORES) % SIDE, index % CORES, lax.axis_index("tensor")


def shift_of(x, y, core):
    along = x * (1 - core) + y * core
    across = y * (1 - core) + x * core
    side = (along % 2 + core) % 2
    far = side * ((8 - across) - 4 * (1 - jnp.minimum(across, 1)))
    return jnp.where(side == 0, across, far)


def owner_of(x, y, core, plane):
    along = x * (1 - core) + y * core
    source = (plane + PLANES - shift_of(x, y, core)) % PLANES
    return 4 * source + 2 * core + along // 2


def main_kernel(
    act_ref, cot_ref, master_ref, one_ref, two_ref, writer_ref,
    gout_ref, mout_ref, pout_ref, base_ref,
    act_own, act_sib, act_t, cot_all, product, acc, asend, arecv, bsend, brecv, zsend, zrecv, gsend,
    m_in, one_in, two_in, msend, psend, codes,
    local_sem, act_sem, cot_sib_sem, zs_sem, zr_sem, fs_sem, fr_sem, as_sem, ar_sem, bs_sem, br_sem,
    ps_sem, pr_sem, gs_sem, gr_sem, ms_sem, mr_sem, qs_sem, qr_sem,
):
    x, y, core, plane = coordinates()
    me = lax.axis_index("dp")
    tokens, _ = cot_ref.shape
    half = act_own.shape[1]
    rows = master_ref.shape[0]
    words = rows // 2
    along = x * (1 - core) + y * core
    across = y * (1 - core) + x * core
    side = (along % 2 + core) % 2
    shift = shift_of(x, y, core)
    sibling = me + 1 - 2 * core
    up = lax.rem(plane + 1, PLANES)
    down = lax.rem(plane + PLANES - 1, PLANES)
    part = tokens // CHUNKS

    def device(a, b):
        return ((a * (1 - core) + b * core) * SIDE + b * (1 - core) + a * core) * CORES + core

    def remote(src, dst, send, recv, dp, at):
        return pltpu.make_async_remote_copy(
            src_ref=src, dst_ref=dst, send_sem=send, recv_sem=recv, device_id=(dp, at), device_id_type=MESH
        )

    def columns_of(which):
        return pl.ds(pl.multiple_of(which * half, 128), half)

    def own_rows(chunk=None):
        if chunk is None:
            return pl.ds(pl.multiple_of(core * tokens, 128), tokens)
        return pl.ds(pl.multiple_of(core * tokens + chunk * part, 128), part)

    loads = [
        pltpu.make_async_copy(act_ref.at[:, columns_of(core)], act_own, local_sem.at[0]),
        pltpu.make_async_copy(cot_ref, cot_all.at[0, own_rows()], local_sem.at[1]),
        pltpu.make_async_copy(master_ref, m_in, local_sem.at[2]),
        pltpu.make_async_copy(one_ref, one_in, local_sem.at[3]),
        pltpu.make_async_copy(two_ref, two_in, local_sem.at[4]),
    ]
    for load in loads:
        load.start()

    barrier = pltpu.get_barrier_semaphore()

    def greet(r, carry):
        pl.semaphore_signal(barrier, inc=1, device_id=(lax.rem(me + r, DP), plane), device_id_type=MESH)
        return carry

    lax.fori_loop(1, DP, greet, 0)
    for at in (up, down):
        pl.semaphore_signal(barrier, inc=1, device_id=(me, at), device_id_type=MESH)

    @pl.when(shift != 0)
    def _():
        pl.semaphore_signal(
            barrier, inc=1, device_id=(me, lax.rem(plane + PLANES - shift, PLANES)), device_id_type=MESH
        )

    pl.semaphore_wait(barrier, DP + 1 + jnp.minimum(shift, 1))

    def z_copy(slot, chunk, direction):
        target = (slot - direction) % PLANES
        rows_here = pl.ds(pl.multiple_of(core * tokens + chunk * part, 128), part)
        if slot == 0:
            src = cot_ref.at[pl.ds(chunk * part, part)]
        else:
            src = cot_all.at[slot, rows_here]
        sem = (target, chunk)
        return remote(
            src, cot_all.at[target, rows_here], zs_sem.at[sem], zr_sem.at[sem], me, up if direction == 1 else down
        )

    def z_last(chunk):
        rows_here = pl.ds(pl.multiple_of(core * tokens + chunk * part, 128), part)
        return remote(
            cot_all.at[5 - 2 * core, rows_here], cot_all.at[4, rows_here], zs_sem.at[4, chunk], zr_sem.at[4, chunk],
            me, lax.rem(plane + 1 - 2 * core + PLANES, PLANES),
        )

    def f_copy(slot):
        src = cot_ref if slot == 0 else cot_all.at[slot, own_rows()]
        return remote(src, cot_all.at[slot, own_rows()], fs_sem.at[slot], fr_sem.at[slot], sibling, plane)

    def f_wait(slot):
        other = pl.ds(pl.multiple_of((1 - core) * tokens, 128), tokens)
        remote(cot_ref, cot_all.at[slot, other], fs_sem.at[slot], fr_sem.at[slot], sibling, plane).wait_recv()

    act_copy = remote(act_ref.at[:, columns_of(1 - core)], act_sib, act_sem.at[0], act_sem.at[1], sibling, plane)
    act_copy.start()
    f_copy(0).start()
    for chunk in range(CHUNKS):
        z_copy(0, chunk, 1).start()
        z_copy(0, chunk, -1).start()

    def transpose_into(source, offset):
        for j in range(half // 128):
            act_t[j * 128 : (j + 1) * 128, pl.ds(pl.multiple_of(offset, 128), tokens)] = source[
                :, j * 128 : (j + 1) * 128
            ].T

    def place_of(owner, split):
        writers = writer_ref[pl.ds(owner, 1), :]
        mine = lax.broadcasted_iota(jnp.int32, (DP, rows), 0) == writers
        below = lax.broadcasted_iota(jnp.int32, (rows, rows), 0) < lax.broadcasted_iota(jnp.int32, (rows, rows), 1)
        before = jnp.dot(
            mine.astype(jnp.bfloat16), below.astype(jnp.bfloat16), preferred_element_type=jnp.float32
        )
        rank = jnp.sum(jnp.where(mine, before, 0.0), axis=0, keepdims=True).astype(jnp.int32)
        if split:
            return (rank >> 4) * (DP * 16) + writers * 16 + (rank & 15)
        return writers * 32 + rank

    def onehot(place, start, count):
        slot = start + lax.broadcasted_iota(jnp.int32, (count, rows), 0)
        return (slot == place).astype(jnp.bfloat16)

    loads[0].wait()
    transpose_into(act_own, core * tokens)
    for load in loads[2:]:
        load.wait()
    e_one = exponent_of(one_in[...])
    code_one = encode(one_in[...], e_one)
    e_two = exponent_of(two_in[...])
    code_two = encode(two_in[...], e_two)
    for k, code in enumerate((code_one, code_two)):
        codes[:, (2 * k) * 256 : (2 * k + 1) * 256] = (code >> 8).astype(jnp.float32).astype(jnp.bfloat16)
        codes[:, (2 * k + 1) * 256 : (2 * k + 2) * 256] = (code & 255).astype(jnp.float32).astype(jnp.bfloat16)
    rest = m_in[...]
    for k in range(3):
        piece = rest.astype(jnp.bfloat16)
        codes[:, (4 + k) * 256 : (5 + k) * 256] = piece
        rest = rest - piece.astype(jnp.float32)
    place_m = place_of(me, False)
    tile = 256
    scale_rows = jnp.concatenate([e_one.astype(jnp.int32)] * 4 + [e_two.astype(jnp.int32)] * 4, axis=0)
    for j in range(1024 // tile):
        packed = jnp.dot(onehot(place_m, j * tile, tile), codes[...], preferred_element_type=jnp.float32)
        q = [packed[:, k * 256 : (k + 1) * 256] for k in range(7)]
        msend[j * 8 : (j + 1) * 8] = (q[4] + q[5] + q[6]).reshape(8, 32, 256)
        word = join((q[0] * 256.0 + q[1]).astype(jnp.int32), (q[2] * 256.0 + q[3]).astype(jnp.int32))
        psend[j * 8 : (j + 1) * 8, 0:32] = word.reshape(8, 32, 256)
        psend[j * 8 : (j + 1) * 8, 32:40] = jnp.broadcast_to(scale_rows[None], (8, 8, 256))

    def m_copy(r):
        to = lax.rem(me + r, DP)
        return remote(msend.at[to], mout_ref.at[me], ms_sem.at[r], mr_sem.at[r], to, plane)

    def p_copy(r):
        to = lax.rem(me + r, DP)
        return remote(psend.at[to], pout_ref.at[me], qs_sem.at[r], qr_sem.at[r], to, plane)

    def m_start(r, carry):
        m_copy(r).start()
        p_copy(r).start()
        return carry

    lax.fori_loop(1, DP, m_start, 0)
    m_self = pltpu.make_async_copy(msend.at[me], mout_ref.at[me], local_sem.at[5])
    p_self = pltpu.make_async_copy(psend.at[me], pout_ref.at[me], local_sem.at[6])
    m_self.start()
    p_self.start()

    act_copy.wait_recv()
    transpose_into(act_sib, (1 - core) * tokens)

    hits = jnp.sum((writer_ref[...] == me).astype(jnp.float32), axis=1, keepdims=True)
    counts = jnp.broadcast_to(hits, (DP, 128)).astype(jnp.bfloat16)
    lower = lax.broadcasted_iota(jnp.int32, (DP + 8, DP), 0) > lax.broadcasted_iota(jnp.int32, (DP + 8, DP), 1)
    base_ref[...] = jnp.dot(lower.astype(jnp.bfloat16), counts, preferred_element_type=jnp.float32).astype(jnp.int32)

    def a_copy(slot, o, a, pair):
        k = lax.rem(along - a + SIDE, SIDE) - 1
        return remote(
            asend.at[slot, o], arecv.at[pair, k], as_sem.at[slot, o], ar_sem.at[pair, k], device(a, across), plane
        )

    def target_of(slot, o):
        return 2 * o + (((1 if slot >= 4 else 0) + core) % 2)

    def write_code(ref, values):
        exponent = exponent_of(values)
        code = encode(values, exponent)
        ref[0:words] = join(code[0:words], code[words:rows])
        ref[words : words + SCALE_ROWS] = jnp.broadcast_to(exponent.astype(jnp.int32), (SCALE_ROWS, values.shape[1]))

    def add_code(ref, total):
        unit = unit_of(ref[words : words + 1, :].astype(jnp.float32))
        word = ref[0:words]
        total[0:words] += high_of(word).astype(jnp.float32) * unit
        total[words:rows] += low_of(word).astype(jnp.float32) * unit

    def multiply(slot, pair):
        for o in range(2):
            a = target_of(slot, o)
            product[...] = jnp.dot(
                act_t[o * rows : (o + 1) * rows, :], cot_all[slot], preferred_element_type=jnp.float32
            )

            @pl.when(a == along)
            def _():
                acc[pair] = product[...]

            @pl.when(a != along)
            def _():
                write_code(asend.at[slot, o], product[...])
                a_copy(slot, o, a, pair).start()

    def b_copy(pair):
        k = lax.rem(across - pair + SIDE, SIDE) - 1
        return remote(bsend.at[pair], brecv.at[k], bs_sem.at[pair], br_sem.at[k], device(along, pair), plane)

    def reduce(pair):
        for k in range(SIDE - 1):
            source = lax.rem(along + k + 1, SIDE)
            remote(
                asend.at[0, 0], arecv.at[pair, k], as_sem.at[0, 0], ar_sem.at[pair, k], device(source, across), plane
            ).wait_recv()
            add_code(arecv.at[pair, k], acc.at[pair])

        @pl.when(across != pair)
        def _():
            write_code(bsend.at[pair], acc[pair])
            b_copy(pair).start()

    def z_wait(slot, chunk):
        rows_here = pl.ds(pl.multiple_of(core * tokens + chunk * part, 128), part)
        remote(
            cot_ref.at[pl.ds(0, part)], cot_all.at[slot, rows_here], zs_sem.at[slot, chunk], zr_sem.at[slot, chunk],
            me, up,
        ).wait_recv()

    loads[1].wait()
    f_wait(0)
    multiply(0, 0)
    for step, (low, high) in enumerate(ORDER):
        for chunk in range(CHUNKS):
            z_wait(low, chunk)
            z_wait(high, chunk)
            if step < 2:
                z_copy(high, chunk, 1).start()
                z_copy(low, chunk, -1).start()
            else:
                z_last(chunk).start()
        f_copy(low).start()
        f_copy(high).start()
        f_wait(low)
        f_wait(high)
        multiply(low, step + 1)
        multiply(high, step + 1)
        if step >= 1:
            reduce(step)
    for chunk in range(CHUNKS):
        z_wait(4, chunk)
    f_copy(4).start()
    reduce(3)
    f_wait(4)
    multiply(4, 0)
    reduce(0)

    for k in range(SIDE - 1):
        source = lax.rem(across + k + 1, SIDE)
        remote(bsend.at[0], brecv.at[k], bs_sem.at[0], br_sem.at[k], device(along, source), plane).wait_recv()
        add_code(brecv.at[k], acc.at[across])

    write_code(zsend, acc[across])
    to_plane = lax.rem(plane + shift, PLANES)

    @pl.when(shift != 0)
    def _():
        move = remote(zsend, zrecv, ps_sem.at[0], pr_sem.at[0], me, to_plane)
        move.start()
        move.wait_recv()

    @pl.when(shift == 0)
    def _():
        zrecv[...] = zsend[...]

    owner = owner_of(x, y, core, plane)
    place_g = place_of(owner, True)
    exponent = zrecv[words : words + SCALE_ROWS]
    word = zrecv[0:words]
    for k, code in enumerate((high_of(word), low_of(word))):
        codes[k * words : (k + 1) * words, 0:256] = (code >> 8).astype(jnp.float32).astype(jnp.bfloat16)
        codes[k * words : (k + 1) * words, 256:512] = (code & 255).astype(jnp.float32).astype(jnp.bfloat16)
    for j in range(2):
        q = []
        for side_of in range(2):
            packed = jnp.dot(
                onehot(place_g, side_of * 512 + j * 256, 256), codes[:, 0:512], preferred_element_type=jnp.float32
            )
            q.append((packed[:, 0:256] * 256.0 + packed[:, 256:512]).astype(jnp.int32))
        gsend[j * 16 : (j + 1) * 16, 0:16] = join(q[0], q[1]).reshape(16, 16, 256)
        gsend[j * 16 : (j + 1) * 16, 16:24] = jnp.broadcast_to(exponent[None], (16, 8, 256))

    def g_copy(r):
        to = lax.rem(me + r, DP)
        return remote(gsend.at[to], gout_ref.at[owner], gs_sem.at[r], gr_sem.at[r], to, plane)

    def g_start(r, carry):
        g_copy(r).start()
        return carry

    lax.fori_loop(1, DP, g_start, 0)
    g_self = pltpu.make_async_copy(gsend.at[me], gout_ref.at[owner], local_sem.at[7])
    g_self.start()

    act_copy.wait_send()
    for slot in (0, 1, 2, 3, 5, 6, 7):
        for chunk in range(CHUNKS):
            if slot in (0, 1, 2):
                z_copy(slot, chunk, -1).wait_send()
            if slot in (0, 7, 6):
                z_copy(slot, chunk, 1).wait_send()
    for chunk in range(CHUNKS):
        z_last(chunk).wait_send()
    for slot in range(PLANES):
        f_copy(slot).wait_send()
        for o in range(2):
            a = target_of(slot, o)

            @pl.when(a != along)
            def _():
                a_copy(slot, o, a, 0).wait_send()

    for pair in range(SIDE):

        @pl.when(across != pair)
        def _():
            b_copy(pair).wait_send()

    @pl.when(shift != 0)
    def _():
        remote(zsend, zrecv, ps_sem.at[0], pr_sem.at[0], me, to_plane).wait_send()

    m_self.wait()
    p_self.wait()
    g_self.wait()

    def finish(r, carry):
        source = lax.rem(me + DP - r, DP)
        from_owner = owner_of(source // (SIDE * CORES), (source // CORES) % SIDE, source % CORES, plane)
        m_copy(r).wait_send()
        p_copy(r).wait_send()
        g_copy(r).wait_send()
        remote(msend.at[0], mout_ref.at[source], ms_sem.at[r], mr_sem.at[r], source, plane).wait_recv()
        remote(psend.at[0], pout_ref.at[source], qs_sem.at[r], qr_sem.at[r], source, plane).wait_recv()
        remote(gsend.at[0], gout_ref.at[from_owner], gs_sem.at[r], gr_sem.at[r], source, plane).wait_recv()
        return carry

    lax.fori_loop(1, DP, finish, 0)


def main_call(activations, cotangent, master, moment_one, moment_two, writers):
    tokens, features = activations.shape
    rows, width = master.shape
    half = features // CORES
    coded = (rows // 2 + SCALE_ROWS, width)
    any_space = pl.BlockSpec(memory_space=pl.ANY)
    vmem = pl.BlockSpec(memory_space=pltpu.VMEM)
    dma = pltpu.SemaphoreType.DMA
    f32, i32, bf16 = jnp.float32, jnp.int32, jnp.bfloat16
    return pl.pallas_call(
        main_kernel,
        name="reduce_and_regroup",
        out_shape=(
            jax.ShapeDtypeStruct((DP, 24, width), i32),
            jax.ShapeDtypeStruct((DP, 32, width), f32),
            jax.ShapeDtypeStruct((DP, 40, width), i32),
            jax.ShapeDtypeStruct((DP + 8, 128), i32),
        ),
        in_specs=[any_space] * 5 + [vmem],
        out_specs=(any_space, any_space, any_space, vmem),
        scratch_shapes=[
            pltpu.VMEM((tokens, half), bf16),
            pltpu.VMEM((tokens, half), bf16),
            pltpu.VMEM((half, 2 * tokens), bf16),
            pltpu.VMEM((PLANES, 2 * tokens, width), bf16),
            pltpu.VMEM((rows, width), f32),
            pltpu.VMEM((SIDE, rows, width), f32),
            pltpu.VMEM((PLANES, 2) + coded, i32),
            pltpu.VMEM((SIDE, SIDE - 1) + coded, i32),
            pltpu.VMEM((SIDE,) + coded, i32),
            pltpu.VMEM((SIDE - 1,) + coded, i32),
            pltpu.VMEM(coded, i32),
            pltpu.VMEM(coded, i32),
            pltpu.VMEM((DP, 24, width), i32),
            pltpu.VMEM((rows, width), f32),
            pltpu.VMEM((rows, width), f32),
            pltpu.VMEM((rows, width), f32),
            pltpu.VMEM((DP, 32, width), f32),
            pltpu.VMEM((DP, 40, width), i32),
            pltpu.VMEM((rows, 7 * width), bf16),
            dma((8,)),
            dma((2,)),
            dma((1,)),
            dma((PLANES, CHUNKS)),
            dma((PLANES, CHUNKS)),
            dma((PLANES,)),
            dma((PLANES,)),
            dma((PLANES, 2)),
            dma((SIDE, SIDE - 1)),
            dma((SIDE,)),
            dma((SIDE - 1,)),
            dma((1,)),
            dma((1,)),
            dma((DP,)),
            dma((DP,)),
            dma((DP,)),
            dma((DP,)),
            dma((DP,)),
            dma((DP,)),
        ],
        compiler_params=pltpu.CompilerParams(
            collective_id=0, has_side_effects=True, vmem_limit_bytes=56 * 1024 * 1024
        ),
        cost_estimate=pl.CostEstimate(
            flops=4 * tokens * features * width * PLANES // 2, bytes_accessed=8 * 1024 * 1024, transcendentals=0
        ),
    )(activations, cotangent, master, moment_one, moment_two, writers)


def finish_kernel(
    base_ref, gradient_ref, master_ref, moments_ref, previous_ref, delta_ref, high_ref, first_ref, second_ref, rows_ref
):
    capacity, width = previous_ref.shape
    pair = capacity // DP
    window = pair + 8
    row = lax.broadcasted_iota(jnp.int32, (window, 3 * width), 0)
    for source in range(DP):
        unit = unit_of(gradient_ref[source, 16:17, :].astype(jnp.float32))
        word = gradient_ref[source, 0:16, :]
        gradient = (
            jnp.concatenate([high_of(word), low_of(word)], axis=0).astype(jnp.float32) * unit
        )
        word = moments_ref[source, 0:32, :]
        one = high_of(word).astype(jnp.float32) * unit_of(moments_ref[source, 32:33, :].astype(jnp.float32))
        two = low_of(word).astype(jnp.float32) * unit_of(moments_ref[source, 36:37, :].astype(jnp.float32))
        block = jnp.concatenate(adam_rows(gradient, master_ref[source], one, two), axis=1)
        start = base_ref[source, 0]
        offset = lax.rem(start, 8)
        aligned = pl.multiple_of(start - offset, 8)
        block = pltpu.roll(jnp.concatenate([block, block[0:8]], axis=0), offset, 0)
        target = rows_ref.at[pl.ds(aligned, window), :]
        target[...] = jnp.where(row >= offset, block, target[...])
    filled = lax.broadcasted_iota(jnp.int32, (capacity, width), 0) < base_ref[DP, 0]
    delta = jnp.where(filled, (rows_ref[0:capacity, 0:width] - previous_ref[...]) / learn_rate, 0.0)
    delta_ref[...] = delta
    high_ref[...] = delta.astype(jnp.bfloat16)
    first_ref[...] = jnp.where(filled, rows_ref[0:capacity, width : 2 * width], 0.0)
    second_ref[...] = jnp.where(filled, rows_ref[0:capacity, 2 * width : 3 * width], 0.0)


def finish_call(base, gradient, master, moments, previous):
    capacity, width = previous.shape
    vmem = pl.BlockSpec(memory_space=pltpu.VMEM)
    return pl.pallas_call(
        finish_kernel,
        name="update_and_place",
        out_shape=(
            jax.ShapeDtypeStruct((capacity, width), jnp.float32),
            jax.ShapeDtypeStruct((capacity, width), jnp.bfloat16),
            jax.ShapeDtypeStruct((capacity, width), jnp.float32),
            jax.ShapeDtypeStruct((capacity, width), jnp.float32),
        ),
        in_specs=[pl.BlockSpec(memory_space=pltpu.SMEM), vmem, vmem, vmem, vmem],
        out_specs=(vmem, vmem, vmem, vmem),
        scratch_shapes=[pltpu.VMEM((capacity + capacity // DP + 8, 3 * width), jnp.float32)],
        compiler_params=pltpu.CompilerParams(vmem_limit_bytes=48 * 1024 * 1024),
    )(base, gradient, master, moments, previous)


def local(activations, cotangent, master, moment_one, moment_two, writer_of, previous):
    writers = writer_of.reshape(DP, master.shape[0])
    gradient, masters, moments, base = main_call(activations, cotangent, master, moment_one, moment_two, writers)
    return finish_call(base, gradient, masters, moments, previous)


def solution(mesh):
    spec = P("dp", "tensor")
    return jax.shard_map(
        local,
        mesh=mesh,
        in_specs=(spec, spec, spec, spec, spec, P(), spec),
        out_specs=(spec, spec, spec, spec),
        check_vma=False,
    )
```

time: 327 us -> 140 us (0.43); the launches traced: 322 us -> 140 us
  waiting for transfers between devices: 229 us -> 0 us
  Pallas kernels: 3.56 us -> 133 us
  starting transfers between devices: 33.7 us -> 0 us
  matrix products: 18.4 us -> 0 us
  between operations: 14.1 us -> 0.66 us
  local copies, waits for them, and re-layouts: 19 us -> 5.88 us
  other arithmetic: 4.32 us -> 0 us
    pallas_call x1 -> x2, Pallas kernels: 3.56 us -> 133 us  [the longest x1 128 us: main_call(): pl.pallas_call(main_kernel, name='reduce_and_regroup', out_shape=(jax.Sha...]
    reduce_scatter x1 -> x0, waiting for transfers between devices: 121 us -> none  [local(): lax.psum_scatter(partial.reshape(owners * row_dev, width), 'dp', scatter_...]
    all_gather x1 -> x0, waiting for transfers between devices: 47.6 us -> none  [local(): columns = lax.all_gather(cotangent, 'tensor', axis=0)]
    all_to_all x1 -> x0, waiting for transfers between devices: 36.6 us -> none  [local(): lax.all_to_all(packed.reshape(owners, pair, 3 * width), 'dp', split_axis=...]
    all_to_all x1 -> x0, starting transfers between devices: 26.9 us -> none  [local(): lax.all_to_all(packed.reshape(owners, pair, 3 * width), 'dp', split_axis=...]
    ppermute x1 -> x0, waiting for transfers between devices: 23.6 us -> none  [local(): gradient = lax.ppermute(piece, ('dp', 'tensor'), perm)]
    dot_general x3 -> x0, matrix products: 18.4 us -> none  [the longest x1 12.7 us: local(): jnp.einsum('tor,ctk->ocrk', activations.reshape(-1, local_owners, row_dev...]
    transpose x1 -> x0, local copies, waits for them, and re-layouts: 16.4 us -> none  [local(): jnp.einsum('tor,ctk->ocrk', activations.reshape(-1, local_owners, row_dev...]
  transfers between devices with their start and end apart: 4 -> 0, of which waited for: 4 -> 0; matrix products, arithmetic and copies ran while one was open for 1% -> 0% of each run, Pallas kernels for 0% -> 0%
where the time goes in v2:
time: 140 us
  Pallas kernels  133 us (95%)
  local copies, waits for them, and re-layouts  5.88 us (4%)
    pallas_call x1, Pallas kernels, main_call(): pl.pallas_call(main_kernel, name='reduce_and_regroup', out_shape=(jax.Sha...  128 us
    pallas_call x1, Pallas kernels, finish_call(): pl.pallas_call(finish_kernel, name='update_and_place', out_shape=(jax.Sha...  5.23 us
    unnamed x10, local copies, waits for them, and re-layouts  4.4 us

profile of v2, /device:TPU:57, one launch (start us, length us, event | category | flops | bytes accessed | tf_op | source)
XLA Modules:
  0.0 139.8 jit_solution(6063694050162096088)
XLA Ops:
  0.6 1.5 %reshape.11.writer_ref = s32[32,512]{1,0:T(8,128)} reshape(s32[16384]{0:T(1024)} %param.12) | data formatting | bytes 131072 | tf_op jit(solution)/shard_map/reshape | solution.py:559
  2.1 0.0 copy-start.1
  2.1 128.0 %reduce_and_regroup.1 = (s32[32,24,256]{2,1,0:T(8,128)}, f32[32,32,256]{2,1,0:T(8,128)}, s32[32,40,256]{2,1,0:T(8,128)}, s32[40,128]{1,0:T(8,128)}) custom-call(bf16[768,2048]{1,0:T(8,128)(2,1)} %act_ref.1, bf16[768,256]{1,0:T(8,128)(2,1)} %cot_ref.1, f32[512,256]{1,0:T(8,128)} %master_ref.1, f32[512,256]{1,0:T(8,128)} %one_ref.1, f32[512,256]{1,0:T(8,128)} %two_ref.1, ...), custom_call_target="tpu_custom_call" | custom-call | flops 6442450944 | bytes 8388608 | tf_op jit(solution)/shard_map/reduce_and_regroup/pallas_call | solution.py:448
  130.2 0.0 copy-done.1
  130.2 0.0 copy-start
  130.2 1.3 copy-done
  131.5 0.0 copy-start.2
  131.5 1.2 copy-done.2
  132.7 0.0 copy-start.3
  132.7 1.1 copy-done.3
  133.8 0.0 copy-start.4
  133.8 0.7 copy-done.4
  134.6 5.2 %update_and_place.1 = (f32[1024,256]{1,0:T(8,128)}, bf16[1024,256]{1,0:T(8,128)(2,1)}, f32[1024,256]{1,0:T(8,128)}, f32[1024,256]{1,0:T(8,128)}) custom-call(s32[40,128]{1,0:T(8,128)S(1)} %copy-done.4, s32[32,24,256]{2,1,0:T(8,128)S(1)} %copy-done.3, f32[32,32,256]{2,1,0:T(8,128)S(1)} %copy-done.2, s32[32,40,256]{2,1,0:T(8,128)S(1)} %copy-done, ...), custom_call_target="tpu_custom_call" | custom-call | tf_op jit(solution)/shard_map/update_and_place/pallas_call | solution.py:542
Async XLA Ops:
  2.1 128.0 %copy-start.1 = (f32[1024,256]{1,0:T(8,128)S(1)}, f32[1024,256]{1,0:T(8,128)}, u32[]{:S(2)}) copy-start(f32[1024,256]{1,0:T(8,128)} %previous_ref.1) | copy-start | bytes 3145732
  130.2 1.3 copy-start
  131.5 1.2 copy-start.2
  132.7 1.1 copy-start.3
  133.8 0.7 copy-start.4

commit v3 on v2

v3 whole, which is shorter than its diff:
```python
import functools

import jax
import jax.numpy as jnp
from jax import lax
from jax.experimental import pallas as pl
from jax.experimental.pallas import tpu as pltpu
from jax.sharding import PartitionSpec as P

learn_rate = 0.01
beta_one = 0.9
beta_two = 0.95
epsilon = 1e-08
decay_rate = 0.1
bias_one = 1.0 - 0.9**10
bias_two = 1.0 - 0.95**10

MESH = pl.DeviceIdType.MESH
SIDE = 4
CORES = 2
DP = SIDE * SIDE * CORES
PLANES = 8
CHUNKS = 4
SCALE_ROWS = 8
TOP = 14.99
ORDER = ((0,), (1, 7), (2, 6), (3, 5), (4,))


def adam_rows(gradient, master, moment_one, moment_two):
    first = beta_one * moment_one + (1.0 - beta_one) * gradient
    second = beta_two * moment_two + (1.0 - beta_two) * gradient * gradient
    step_dir = first / bias_one / (jnp.sqrt(second / bias_two) + epsilon) + decay_rate * master
    return (master - learn_rate * step_dir, first, second)


def exponent_of(values):
    most = jnp.max(jnp.abs(values), axis=0, keepdims=True)
    return jnp.ceil(jnp.log2(jnp.maximum(most, 1e-30)))


def encode(values, exponent):
    return jnp.round(values * jnp.exp2(TOP - exponent)).astype(jnp.int32)


def unit_of(exponent):
    return 1.0 / jnp.exp2(TOP - exponent)


def join(high, low):
    return (high << 16) | (low & 0xFFFF)


def high_of(word):
    return word >> 16


def low_of(word):
    return (word << 16) >> 16


def coordinates():
    index = lax.axis_index("dp")
    return index // (SIDE * CORES), (index // CORES) % SIDE, index % CORES, lax.axis_index("tensor")


def axes_of(x, y, core):
    return x * (1 - core) + y * core, y * (1 - core) + x * core


def pair_of(slot):
    return slot if slot < 4 else (8 - slot) % 4


def shifts_of(across):
    return across, 8 - across - 4 * (1 - jnp.minimum(across, 1))


def main_kernel(
    act_ref, cot_ref, master_ref, one_ref, two_ref, writer_ref,
    gout_ref, mout_ref, pout_ref, base_ref,
    act_own, act_sib, act_t, cot_all, product, osend, orecv, nsend, nrecv, bsend, brecv, zsend, zrecv, gsend,
    m_in, one_in, two_in, msend, psend, codes,
    local_sem, act_sem, cot_sib_sem, zs_sem, zr_sem, fs_sem, fr_sem, os_sem, or_sem, ns_sem, nr_sem, bs_sem, br_sem,
    ps_sem, pr_sem, gs_sem, gr_sem, ms_sem, mr_sem, qs_sem, qr_sem,
):
    x, y, core, plane = coordinates()
    me = lax.axis_index("dp")
    tokens, _ = cot_ref.shape
    half = act_own.shape[1]
    rows = master_ref.shape[0]
    words = rows // 2
    along, across = axes_of(x, y, core)
    shifts = shifts_of(across)
    sibling = me + 1 - 2 * core
    up = lax.rem(plane + 1, PLANES)
    down = lax.rem(plane + PLANES - 1, PLANES)
    part = tokens // CHUNKS

    def device(a, b):
        return ((a * (1 - core) + b * core) * SIDE + b * (1 - core) + a * core) * CORES + core

    right = device(lax.rem(along + 1, SIDE), across)
    left = device(lax.rem(along + SIDE - 1, SIDE), across)

    def remote(src, dst, send, recv, dp, at):
        return pltpu.make_async_remote_copy(
            src_ref=src, dst_ref=dst, send_sem=send, recv_sem=recv, device_id=(dp, at), device_id_type=MESH
        )

    def columns_of(which):
        return pl.ds(pl.multiple_of(which * half, 128), half)

    def own_rows(chunk=None):
        if chunk is None:
            return pl.ds(pl.multiple_of(core * tokens, 128), tokens)
        return pl.ds(pl.multiple_of(core * tokens + chunk * part, 64), part)

    loads = [
        pltpu.make_async_copy(act_ref.at[:, columns_of(core)], act_own, local_sem.at[0]),
        pltpu.make_async_copy(cot_ref, cot_all.at[0, own_rows()], local_sem.at[1]),
        pltpu.make_async_copy(master_ref, m_in, local_sem.at[2]),
        pltpu.make_async_copy(one_ref, one_in, local_sem.at[3]),
        pltpu.make_async_copy(two_ref, two_in, local_sem.at[4]),
    ]
    for load in loads:
        load.start()

    barrier = pltpu.get_barrier_semaphore()

    def greet(r, carry):
        pl.semaphore_signal(barrier, inc=1, device_id=(lax.rem(me + r, DP), plane), device_id_type=MESH)
        return carry

    lax.fori_loop(1, DP, greet, 0)
    for at in (up, down):
        pl.semaphore_signal(barrier, inc=1, device_id=(me, at), device_id_type=MESH)

    pl.semaphore_signal(
        barrier, inc=1, device_id=(me, lax.rem(plane + PLANES - shifts[1], PLANES)), device_id_type=MESH
    )

    @pl.when(across != 0)
    def _():
        pl.semaphore_signal(
            barrier, inc=1, device_id=(me, lax.rem(plane + PLANES - across, PLANES)), device_id_type=MESH
        )

    pl.semaphore_wait(barrier, DP + 2 + jnp.minimum(across, 1))

    def z_copy(slot, chunk, direction):
        target = (slot - direction) % PLANES
        rows_here = pl.ds(pl.multiple_of(core * tokens + chunk * part, 64), part)
        if slot == 0:
            src = cot_ref.at[pl.ds(chunk * part, part)]
        else:
            src = cot_all.at[slot, rows_here]
        sem = (target, chunk)
        return remote(
            src, cot_all.at[target, rows_here], zs_sem.at[sem], zr_sem.at[sem], me, up if direction == 1 else down
        )

    def z_last(chunk):
        rows_here = pl.ds(pl.multiple_of(core * tokens + chunk * part, 64), part)
        return remote(
            cot_all.at[5 - 2 * core, rows_here], cot_all.at[4, rows_here], zs_sem.at[4, chunk], zr_sem.at[4, chunk],
            me, lax.rem(plane + 1 - 2 * core + PLANES, PLANES),
        )

    def f_copy(slot, chunk):
        rows_here = own_rows(chunk)
        src = cot_ref.at[pl.ds(chunk * part, part)] if slot == 0 else cot_all.at[slot, rows_here]
        sem = (slot, chunk)
        return remote(src, cot_all.at[slot, rows_here], fs_sem.at[sem], fr_sem.at[sem], sibling, plane)

    def f_wait(slot):
        for chunk in range(CHUNKS):
            other = pl.ds(pl.multiple_of((1 - core) * tokens + chunk * part, 64), part)
            sem = (slot, chunk)
            remote(
                cot_ref.at[pl.ds(0, part)], cot_all.at[slot, other], fs_sem.at[sem], fr_sem.at[sem], sibling, plane
            ).wait_recv()

    act_copy = remote(act_ref.at[:, columns_of(1 - core)], act_sib, act_sem.at[0], act_sem.at[1], sibling, plane)
    for chunk in range(CHUNKS):
        z_copy(0, chunk, 1).start()
        z_copy(0, chunk, -1).start()
    act_copy.start()
    for chunk in range(CHUNKS):
        f_copy(0, chunk).start()

    def z_wait(slot, chunk):
        rows_here = pl.ds(pl.multiple_of(core * tokens + chunk * part, 64), part)
        remote(
            cot_ref.at[pl.ds(0, part)], cot_all.at[slot, rows_here], zs_sem.at[slot, chunk], zr_sem.at[slot, chunk],
            me, up,
        ).wait_recv()

    def service(step, chunk):
        for slot in ORDER[step]:
            z_wait(slot, chunk)
        if step < 3:
            z_copy(ORDER[step][1], chunk, 1).start()
            z_copy(ORDER[step][0], chunk, -1).start()
        elif step == 3:
            z_last(chunk).start()
        for slot in ORDER[step]:
            f_copy(slot, chunk).start()

    def transpose_into(source, offset):
        for j in range(half // 128):
            act_t[j * 128 : (j + 1) * 128, pl.ds(pl.multiple_of(offset, 128), tokens)] = source[
                :, j * 128 : (j + 1) * 128
            ].T

    def place_of(owner, split):
        writers = writer_ref[pl.ds(owner, 1), :]
        mine = lax.broadcasted_iota(jnp.int32, (DP, rows), 0) == writers
        below = lax.broadcasted_iota(jnp.int32, (rows, rows), 0) < lax.broadcasted_iota(jnp.int32, (rows, rows), 1)
        before = jnp.dot(
            mine.astype(jnp.bfloat16), below.astype(jnp.bfloat16), preferred_element_type=jnp.float32
        )
        rank = jnp.sum(jnp.where(mine, before, 0.0), axis=0, keepdims=True).astype(jnp.int32)
        if split:
            return (rank >> 4) * (DP * 16) + writers * 16 + (rank & 15)
        return writers * 32 + rank

    def onehot(place, start, count):
        slot = start + lax.broadcasted_iota(jnp.int32, (count, rows), 0)
        return (slot == place).astype(jnp.bfloat16)

    loads[0].wait()
    transpose_into(act_own, core * tokens)
    for load in loads[2:]:
        load.wait()
    e_one = exponent_of(one_in[...])
    code_one = encode(one_in[...], e_one)
    e_two = exponent_of(two_in[...])
    code_two = encode(two_in[...], e_two)
    for k, code in enumerate((code_one, code_two)):
        codes[:, (2 * k) * 256 : (2 * k + 1) * 256] = (code >> 8).astype(jnp.float32).astype(jnp.bfloat16)
        codes[:, (2 * k + 1) * 256 : (2 * k + 2) * 256] = (code & 255).astype(jnp.float32).astype(jnp.bfloat16)
    rest = m_in[...]
    for k in range(3):
        piece = rest.astype(jnp.bfloat16)
        codes[:, (4 + k) * 256 : (5 + k) * 256] = piece
        rest = rest - piece.astype(jnp.float32)
    place_m = place_of(me, False)
    tile = 256
    scale_rows = jnp.concatenate([e_one.astype(jnp.int32)] * 4 + [e_two.astype(jnp.int32)] * 4, axis=0)
    for j in range(1024 // tile):
        packed = jnp.dot(onehot(place_m, j * tile, tile), codes[...], preferred_element_type=jnp.float32)
        q = [packed[:, k * 256 : (k + 1) * 256] for k in range(7)]
        msend[j * 8 : (j + 1) * 8] = (q[4] + q[5] + q[6]).reshape(8, 32, 256)
        word = join((q[0] * 256.0 + q[1]).astype(jnp.int32), (q[2] * 256.0 + q[3]).astype(jnp.int32))
        psend[j * 8 : (j + 1) * 8, 0:32] = word.reshape(8, 32, 256)
        psend[j * 8 : (j + 1) * 8, 32:40] = jnp.broadcast_to(scale_rows[None], (8, 8, 256))

    def m_copy(r):
        to = lax.rem(me + r, DP)
        return remote(msend.at[to], mout_ref.at[me], ms_sem.at[r], mr_sem.at[r], to, plane)

    def p_copy(r):
        to = lax.rem(me + r, DP)
        return remote(psend.at[to], pout_ref.at[me], qs_sem.at[r], qr_sem.at[r], to, plane)

    def m_start(r, carry):
        m_copy(r).start()
        return carry

    lax.fori_loop(1, DP, m_start, 0)
    m_self = pltpu.make_async_copy(msend.at[me], mout_ref.at[me], local_sem.at[5])
    p_self = pltpu.make_async_copy(psend.at[me], pout_ref.at[me], local_sem.at[6])
    m_self.start()
    p_self.start()

    service(1, 0)
    act_copy.wait_recv()
    transpose_into(act_sib, (1 - core) * tokens)

    hits = jnp.sum((writer_ref[...] == me).astype(jnp.float32), axis=1, keepdims=True)
    counts = jnp.broadcast_to(hits, (DP, 128)).astype(jnp.bfloat16)
    lower = lax.broadcasted_iota(jnp.int32, (DP + 8, DP), 0) > lax.broadcasted_iota(jnp.int32, (DP + 8, DP), 1)
    base_ref[...] = jnp.dot(lower.astype(jnp.bfloat16), counts, preferred_element_type=jnp.float32).astype(jnp.int32)

    def write_code(values, *refs):
        exponent = exponent_of(values)
        code = encode(values, exponent)
        word = join(code[0:words], code[words:rows])
        count = words // len(refs)
        for i, ref in enumerate(refs):
            ref[0:count] = word[i * count : (i + 1) * count]
            ref[count : count + SCALE_ROWS] = jnp.broadcast_to(
                exponent.astype(jnp.int32), (SCALE_ROWS, values.shape[1])
            )

    def add_code(ref, total, start, count):
        unit = unit_of(ref[count : count + 1, :].astype(jnp.float32))
        word = ref[0:count]
        total[start : start + count] += high_of(word).astype(jnp.float32) * unit
        total[words + start : words + start + count] += low_of(word).astype(jnp.float32) * unit

    def far_copy(slot, i):
        return remote(
            osend.at[slot, i], orecv.at[slot, i], os_sem.at[slot, i], or_sem.at[slot, i], left if i else right, plane
        )

    def near_copy(slot, i):
        return remote(
            nsend.at[slot, i], nrecv.at[slot, i], ns_sem.at[slot, i], nr_sem.at[slot, i], left if i else right, plane
        )

    def b_copy(slot):
        k = lax.rem(across - pair_of(slot) + SIDE, SIDE) - 1
        j = 0 if slot < 4 else 1
        return remote(
            bsend.at[slot], brecv.at[j, k], bs_sem.at[slot], br_sem.at[j, k], device(along, pair_of(slot)), plane
        )

    def multiply(slot):
        for o in range(2):
            block = jnp.dot(
                act_t[o * rows : (o + 1) * rows, :], cot_all[slot], preferred_element_type=jnp.float32
            )
            product[slot, 2 * o] = block[:, 0:128]
            product[slot, 2 * o + 1] = block[:, 128:256]
        write_code(product[slot, lax.rem(along + 2, SIDE)], osend.at[slot, 0], osend.at[slot, 1])
        far_copy(slot, 0).start()
        far_copy(slot, 1).start()

    def pass_on(slot):
        for i, turn in ((0, 1), (1, SIDE - 1)):
            target = lax.rem(along + turn, SIDE)
            far_copy(slot, i).wait_recv()
            add_code(orecv.at[slot, i], product.at[slot, target], i * (words // 2), words // 2)
            write_code(product[slot, target], nsend.at[slot, i])
            near_copy(slot, i).start()

    def reduce(slot):
        for i in range(2):
            near_copy(slot, i).wait_recv()
            add_code(nrecv.at[slot, i], product.at[slot, along], 0, words)

        @pl.when(across != pair_of(slot))
        def _():
            write_code(product[slot, along], bsend.at[slot])
            b_copy(slot).start()

    def p_move(j):
        return remote(
            zsend.at[j], zrecv.at[j], ps_sem.at[j], pr_sem.at[j], me, lax.rem(plane + shifts[j], PLANES)
        )

    def whole(j):
        slot = shifts[j]
        for k in range(SIDE - 1):
            source = lax.rem(across + k + 1, SIDE)
            remote(
                bsend.at[0], brecv.at[j, k], bs_sem.at[0], br_sem.at[j, k], device(along, source), plane
            ).wait_recv()
            add_code(brecv.at[j, k], product.at[slot, along], 0, words)
        write_code(product[slot, along], zsend.at[j])

    loads[1].wait()
    f_wait(0)
    multiply(0)
    for chunk in range(1, CHUNKS):
        service(1, chunk)
    for step in (1, 2, 3):
        f_wait(ORDER[step][0])
        multiply(ORDER[step][0])
        service(step + 1, 0)
        f_wait(ORDER[step][1])
        multiply(ORDER[step][1])
        service(step + 1, 1)
        for slot in ORDER[step - 1]:
            pass_on(slot)
        service(step + 1, 2)
        if step >= 2:
            for slot in ORDER[step - 2]:
                reduce(slot)
        service(step + 1, 3)
    f_wait(4)
    multiply(4)
    for slot in ORDER[3]:
        pass_on(slot)
    for slot in ORDER[2]:
        reduce(slot)
    pass_on(4)
    for slot in ORDER[3] + ORDER[4]:
        reduce(slot)

    def p_start(r, carry):
        p_copy(r).start()
        return carry

    lax.fori_loop(1, DP, p_start, 0)

    whole(0)

    @pl.when(across != 0)
    def _():
        p_move(0).start()

    whole(1)
    p_move(1).start()

    owners = [4 * lax.rem(plane + PLANES - shift, PLANES) + 2 * core + along // 2 for shift in shifts]
    for j in range(2):
        place_g = place_of(owners[j], True)
        if j == 0:

            @pl.when(across != 0)
            def _():
                p_move(0).wait_recv()

            @pl.when(across == 0)
            def _():
                zrecv[0] = zsend[0]

        else:
            p_move(1).wait_recv()
        exponent = zrecv[j, words : words + SCALE_ROWS]
        word = zrecv[j, 0:words]
        for k, code in enumerate((high_of(word), low_of(word))):
            codes[k * words : (k + 1) * words, 0:128] = (code >> 8).astype(jnp.float32).astype(jnp.bfloat16)
            codes[k * words : (k + 1) * words, 128:256] = (code & 255).astype(jnp.float32).astype(jnp.bfloat16)
        for i in range(2):
            q = []
            for side_of in range(2):
                packed = jnp.dot(
                    onehot(place_g, side_of * 512 + i * 256, 256), codes[:, 0:256], preferred_element_type=jnp.float32
                )
                q.append((packed[:, 0:128] * 256.0 + packed[:, 128:256]).astype(jnp.int32))
            gsend[i * 16 : (i + 1) * 16, j, 0:16] = join(q[0], q[1]).reshape(16, 16, 128)
            gsend[i * 16 : (i + 1) * 16, j, 16:24] = jnp.broadcast_to(exponent[None], (16, 8, 128))

    def g_copy(r):
        to = lax.rem(me + r, DP)
        return remote(gsend.at[to], gout_ref.at[me], gs_sem.at[r], gr_sem.at[r], to, plane)

    def g_start(r, carry):
        g_copy(r).start()
        return carry

    lax.fori_loop(1, DP, g_start, 0)
    g_self = pltpu.make_async_copy(gsend.at[me], gout_ref.at[me], local_sem.at[7])
    g_self.start()

    act_copy.wait_send()
    for slot in (0, 1, 2, 3, 5, 6, 7):
        for chunk in range(CHUNKS):
            if slot in (0, 1, 2):
                z_copy(slot, chunk, -1).wait_send()
            if slot in (0, 7, 6):
                z_copy(slot, chunk, 1).wait_send()
    for chunk in range(CHUNKS):
        z_last(chunk).wait_send()
    for slot in range(PLANES):
        for chunk in range(CHUNKS):
            f_copy(slot, chunk).wait_send()
        for i in range(2):
            far_copy(slot, i).wait_send()
            near_copy(slot, i).wait_send()

        @pl.when(across != pair_of(slot))
        def _():
            b_copy(slot).wait_send()

    @pl.when(across != 0)
    def _():
        p_move(0).wait_send()

    p_move(1).wait_send()
    m_self.wait()
    p_self.wait()
    g_self.wait()

    def finish(r, carry):
        source = lax.rem(me + DP - r, DP)
        m_copy(r).wait_send()
        p_copy(r).wait_send()
        g_copy(r).wait_send()
        remote(msend.at[0], mout_ref.at[source], ms_sem.at[r], mr_sem.at[r], source, plane).wait_recv()
        remote(psend.at[0], pout_ref.at[source], qs_sem.at[r], qr_sem.at[r], source, plane).wait_recv()
        remote(gsend.at[0], gout_ref.at[source], gs_sem.at[r], gr_sem.at[r], source, plane).wait_recv()
        return carry

    lax.fori_loop(1, DP, finish, 0)


def main_call(activations, cotangent, master, moment_one, moment_two, writers):
    tokens, features = activations.shape
    rows, width = master.shape
    half = features // CORES
    side = width // 2
    coded = (rows // 2 + SCALE_ROWS, side)
    any_space = pl.BlockSpec(memory_space=pl.ANY)
    vmem = pl.BlockSpec(memory_space=pltpu.VMEM)
    dma = pltpu.SemaphoreType.DMA
    f32, i32, bf16 = jnp.float32, jnp.int32, jnp.bfloat16
    return pl.pallas_call(
        main_kernel,
        name="reduce_and_regroup",
        out_shape=(
            jax.ShapeDtypeStruct((DP, 2, 24, side), i32),
            jax.ShapeDtypeStruct((DP, 32, width), f32),
            jax.ShapeDtypeStruct((DP, 40, width), i32),
            jax.ShapeDtypeStruct((DP + 8, 128), i32),
        ),
        in_specs=[any_space] * 5 + [vmem],
        out_specs=(any_space, any_space, any_space, vmem),
        scratch_shapes=[
            pltpu.VMEM((tokens, half), bf16),
            pltpu.VMEM((tokens, half), bf16),
            pltpu.VMEM((half, 2 * tokens), bf16),
            pltpu.VMEM((PLANES, 2 * tokens, width), bf16),
            pltpu.VMEM((PLANES, SIDE, rows, side), f32),
            pltpu.VMEM((PLANES, 2, rows // 4 + SCALE_ROWS, side), i32),
            pltpu.VMEM((PLANES, 2, rows // 4 + SCALE_ROWS, side), i32),
            pltpu.VMEM((PLANES, 2) + coded, i32),
            pltpu.VMEM((PLANES, 2) + coded, i32),
            pltpu.VMEM((PLANES,) + coded, i32),
            pltpu.VMEM((2, SIDE - 1) + coded, i32),
            pltpu.VMEM((2,) + coded, i32),
            pltpu.VMEM((2,) + coded, i32),
            pltpu.VMEM((DP, 2, 24, side), i32),
            pltpu.VMEM((rows, width), f32),
            pltpu.VMEM((rows, width), f32),
            pltpu.VMEM((rows, width), f32),
            pltpu.VMEM((DP, 32, width), f32),
            pltpu.VMEM((DP, 40, width), i32),
            pltpu.VMEM((rows, 7 * width), bf16),
            dma((8,)),
            dma((2,)),
            dma((1,)),
            dma((PLANES, CHUNKS)),
            dma((PLANES, CHUNKS)),
            dma((PLANES, CHUNKS)),
            dma((PLANES, CHUNKS)),
            dma((PLANES, 2)),
            dma((PLANES, 2)),
            dma((PLANES, 2)),
            dma((PLANES, 2)),
            dma((PLANES,)),
            dma((2, SIDE - 1)),
            dma((2,)),
            dma((2,)),
            dma((DP,)),
            dma((DP,)),
            dma((DP,)),
            dma((DP,)),
            dma((DP,)),
            dma((DP,)),
        ],
        compiler_params=pltpu.CompilerParams(
            collective_id=0, has_side_effects=True, vmem_limit_bytes=56 * 1024 * 1024
        ),
        cost_estimate=pl.CostEstimate(
            flops=4 * tokens * features * width * PLANES // 2, bytes_accessed=8 * 1024 * 1024, transcendentals=0
        ),
    )(activations, cotangent, master, moment_one, moment_two, writers)


def source_of(owner, part, plane):
    slot = lax.rem(plane + PLANES - owner // 4, PLANES)
    late = slot // 4
    across = jnp.where(late == 0, slot, lax.rem(PLANES - slot, 4))
    core = (owner // 2) % 2
    x, y = axes_of(2 * (owner % 2) + part, across, core)
    return (x * SIDE + y) * CORES + core, late


def finish_kernel(
    base_ref, gradient_hbm, master_hbm, moments_hbm, previous_hbm,
    delta_ref, high_ref, first_ref, second_ref,
    gradient_ref, master_ref, moments_ref, previous_ref, rows_ref, sem,
):
    loads = [
        pltpu.make_async_copy(moments_hbm, moments_ref, sem.at[0]),
        pltpu.make_async_copy(master_hbm, master_ref, sem.at[1]),
        pltpu.make_async_copy(gradient_hbm, gradient_ref, sem.at[2]),
        pltpu.make_async_copy(previous_hbm, previous_ref, sem.at[3]),
    ]
    for load in loads:
        load.start()
    plane = lax.axis_index("tensor")
    capacity, width = previous_ref.shape
    pair = capacity // DP
    window = pair + 8
    row = lax.broadcasted_iota(jnp.int32, (window, 3 * width), 0)
    for load in loads[:3]:
        load.wait()
    for owner in range(DP):
        parts = []
        for part in range(2):
            source, late = source_of(owner, part, plane)
            unit = unit_of(gradient_ref[source, late, 16:17, :].astype(jnp.float32))
            word = gradient_ref[source, late, 0:16, :]
            parts.append(jnp.concatenate([high_of(word), low_of(word)], axis=0).astype(jnp.float32) * unit)
        gradient = jnp.concatenate(parts, axis=1)
        word = moments_ref[owner, 0:32, :]
        one = high_of(word).astype(jnp.float32) * unit_of(moments_ref[owner, 32:33, :].astype(jnp.float32))
        two = low_of(word).astype(jnp.float32) * unit_of(moments_ref[owner, 36:37, :].astype(jnp.float32))
        block = jnp.concatenate(adam_rows(gradient, master_ref[owner], one, two), axis=1)
        start = base_ref[owner, 0]
        offset = lax.rem(start, 8)
        aligned = pl.multiple_of(start - offset, 8)
        block = pltpu.roll(jnp.concatenate([block, block[0:8]], axis=0), offset, 0)
        target = rows_ref.at[pl.ds(aligned, window), :]
        target[...] = jnp.where(row >= offset, block, target[...])
    loads[3].wait()
    filled = lax.broadcasted_iota(jnp.int32, (capacity, width), 0) < base_ref[DP, 0]
    delta = jnp.where(filled, (rows_ref[0:capacity, 0:width] - previous_ref[...]) / learn_rate, 0.0)
    delta_ref[...] = delta
    high_ref[...] = delta.astype(jnp.bfloat16)
    first_ref[...] = jnp.where(filled, rows_ref[0:capacity, width : 2 * width], 0.0)
    second_ref[...] = jnp.where(filled, rows_ref[0:capacity, 2 * width : 3 * width], 0.0)


def finish_call(base, gradient, master, moments, previous):
    capacity, width = previous.shape
    vmem = pl.BlockSpec(memory_space=pltpu.VMEM)
    any_space = pl.BlockSpec(memory_space=pl.ANY)
    return pl.pallas_call(
        finish_kernel,
        name="update_and_place",
        out_shape=(
            jax.ShapeDtypeStruct((capacity, width), jnp.float32),
            jax.ShapeDtypeStruct((capacity, width), jnp.bfloat16),
            jax.ShapeDtypeStruct((capacity, width), jnp.float32),
            jax.ShapeDtypeStruct((capacity, width), jnp.float32),
        ),
        in_specs=[pl.BlockSpec(memory_space=pltpu.SMEM)] + [any_space] * 4,
        out_specs=(vmem, vmem, vmem, vmem),
        scratch_shapes=[
            pltpu.VMEM(gradient.shape, gradient.dtype),
            pltpu.VMEM(master.shape, master.dtype),
            pltpu.VMEM(moments.shape, moments.dtype),
            pltpu.VMEM(previous.shape, previous.dtype),
            pltpu.VMEM((capacity + capacity // DP + 8, 3 * width), jnp.float32),
            pltpu.SemaphoreType.DMA((4,)),
        ],
        compiler_params=pltpu.CompilerParams(vmem_limit_bytes=60 * 1024 * 1024),
    )(base, gradient, master, moments, previous)


def local(activations, cotangent, master, moment_one, moment_two, writer_of, previous):
    writers = writer_of.reshape(DP, master.shape[0])
    gradient, masters, moments, base = main_call(activations, cotangent, master, moment_one, moment_two, writers)
    return finish_call(base, gradient, masters, moments, previous)


def solution(mesh):
    spec = P("dp", "tensor")
    return jax.shard_map(
        local,
        mesh=mesh,
        in_specs=(spec, spec, spec, spec, spec, P(), spec),
        out_specs=(spec, spec, spec, spec),
        check_vma=False,
    )
```

time: 140 us -> 110 us (0.79)
  Pallas kernels: 133 us -> 107 us
  local copies, waits for them, and re-layouts: 5.88 us -> 1.48 us
    pallas_call x1, Pallas kernels: 128 us -> 99.7 us  [main_call(): pl.pallas_call(main_kernel, name='reduce_and_regroup', out_shape=(jax.Sha...]
    unnamed x10 -> x0, local copies, waits for them, and re-layouts: 4.4 us -> none
    pallas_call x1, Pallas kernels: 5.23 us -> 7.12 us  [finish_call(): pl.pallas_call(finish_kernel, name='update_and_place', out_shape=(jax.Sha...]
where the time goes in v3:
time: 110 us; the launch traced here: 109 us
  Pallas kernels  107 us (97%)
  local copies, waits for them, and re-layouts  1.48 us (1%)
    pallas_call x1, Pallas kernels, main_call(): pl.pallas_call(main_kernel, name='reduce_and_regroup', out_shape=(jax.Sha...  99.7 us
    pallas_call x1, Pallas kernels, finish_call(): pl.pallas_call(finish_kernel, name='update_and_place', out_shape=(jax.Sha...  7.12 us

profile of v3, /device:TPU:57, one launch (start us, length us, event | category | flops | bytes accessed | tf_op | source)
XLA Modules:
  0.0 109.1 jit_solution(5230497819845079104)
XLA Ops:
  0.6 1.5 %reshape.11.writer_ref = s32[32,512]{1,0:T(8,128)} reshape(s32[16384]{0:T(1024)} %param.12) | data formatting | bytes 131072 | tf_op jit(solution)/shard_map/reshape | solution.py:648
  2.1 99.7 %reduce_and_regroup.1 = (s32[32,2,24,128]{3,2,1,0:T(8,128)}, f32[32,32,256]{2,1,0:T(8,128)}, s32[32,40,256]{2,1,0:T(8,128)}, s32[40,128]{1,0:T(8,128)}) custom-call(bf16[768,2048]{1,0:T(8,128)(2,1)} %act_ref.1, bf16[768,256]{1,0:T(8,128)(2,1)} %cot_ref.1, f32[512,256]{1,0:T(8,128)} %master_ref.1, f32[512,256]{1,0:T(8,128)} %one_ref.1, f32[512,256]{1,0:T(8,128)} %two_ref.1, ...), custom_call_target="tpu_custom_call" | custom-call | flops 6442450944 | bytes 8388608 | tf_op jit(solution)/shard_map/reduce_and_regroup/pallas_call | solution.py:501
  101.8 7.1 %update_and_place.1 = (f32[1024,256]{1,0:T(8,128)}, bf16[1024,256]{1,0:T(8,128)(2,1)}, f32[1024,256]{1,0:T(8,128)}, f32[1024,256]{1,0:T(8,128)}) custom-call(s32[40,128]{1,0:T(8,128)} %get-tuple-element.8.base_ref, s32[32,2,24,128]{3,2,1,0:T(8,128)} %get-tuple-element.9.gradient_hbm, f32[32,32,256]{2,1,0:T(8,128)} %get-tuple-element.10.master_hbm, ...), custom_call_target="tpu_custom_call" | custom-call | tf_op jit(solution)/shard_map/update_and_place/pallas_call | solution.py:624

commit v4 on v3

--- a/solution.py
+++ b/solution.py
@@ -23,14 +23,21 @@
 CHUNKS = 4
 SCALE_ROWS = 8
 TOP = 14.99
+PERIOD = 0.625
+STEP = PERIOD / 2**20
+OFFSET = 128
+SPREAD = ((1, 4), (4, 7), (7, 10), (10, 13), (13, 15), (15, 17), (17, 19), (19, 21), (21, 22), (22, 23), (23, 23), (23, 23), (23, 23), (23, 23), (23, 23), (23, 23))
 ORDER = ((0,), (1, 7), (2, 6), (3, 5), (4,))
 
 
-def adam_rows(gradient, master, moment_one, moment_two):
+def moments_of(gradient, moment_one, moment_two):
     first = beta_one * moment_one + (1.0 - beta_one) * gradient
     second = beta_two * moment_two + (1.0 - beta_two) * gradient * gradient
-    step_dir = first / bias_one / (jnp.sqrt(second / bias_two) + epsilon) + decay_rate * master
-    return (master - learn_rate * step_dir, first, second)
+    return first, second
+
+
+def step_of(first, second, master):
+    return first / bias_one / (jnp.sqrt(second / bias_two) + epsilon) + decay_rate * master
 
 
 def exponent_of(values):
@@ -46,6 +53,10 @@
     return 1.0 / jnp.exp2(TOP - exponent)
 
 
+def within_period(values):
+    return values - jnp.floor(values * (1.0 / PERIOD)) * PERIOD
+
+
 def join(high, low):
     return (high << 16) | (low & 0xFFFF)
 
@@ -76,12 +87,12 @@
 
 
 def main_kernel(
-    act_ref, cot_ref, master_ref, one_ref, two_ref, writer_ref,
-    gout_ref, mout_ref, pout_ref, base_ref,
+    act_ref, cot_ref, master_ref, one_ref, two_ref, writer_flat,
+    gout_ref, pout_ref, base_ref,
     act_own, act_sib, act_t, cot_all, product, osend, orecv, nsend, nrecv, bsend, brecv, zsend, zrecv, gsend,
-    m_in, one_in, two_in, msend, psend, codes,
+    m_in, one_in, two_in, psend, codes, writer_ref,
     local_sem, act_sem, cot_sib_sem, zs_sem, zr_sem, fs_sem, fr_sem, os_sem, or_sem, ns_sem, nr_sem, bs_sem, br_sem,
-    ps_sem, pr_sem, gs_sem, gr_sem, ms_sem, mr_sem, qs_sem, qr_sem,
+    ps_sem, pr_sem, gs_sem, gr_sem, qs_sem, qr_sem,
 ):
     x, y, core, plane = coordinates()
     me = lax.axis_index("dp")
@@ -145,6 +156,22 @@
             barrier, inc=1, device_id=(me, lax.rem(plane + PLANES - across, PLANES)), device_id_type=MESH
         )
 
+    def place_of(owner, split):
+        writers = writer_ref[pl.ds(owner, 1), :]
+        mine = lax.broadcasted_iota(jnp.int32, (DP, rows), 0) == writers
+        below = lax.broadcasted_iota(jnp.int32, (rows, rows), 0) < lax.broadcasted_iota(jnp.int32, (rows, rows), 1)
+        before = jnp.dot(
+            mine.astype(jnp.bfloat16), below.astype(jnp.bfloat16), preferred_element_type=jnp.float32
+        )
+        rank = jnp.sum(jnp.where(mine, before, 0.0), axis=0, keepdims=True).astype(jnp.int32)
+        if split:
+            return (rank >> 4) * (DP * 16) + writers * 16 + (rank & 15)
+        return writers * 32 + rank
+
+    for k in range(rows // 128):
+        writer_ref[:, k * 128 : (k + 1) * 128] = writer_flat[pl.ds(k, DP, stride=rows // 128), :]
+
+    place_m = place_of(me, False)
     pl.semaphore_wait(barrier, DP + 2 + jnp.minimum(across, 1))
 
     def z_copy(slot, chunk, direction):
@@ -195,6 +222,10 @@
             me, up,
         ).wait_recv()
 
+    def p_copy(r):
+        to = lax.rem(me + r, DP)
+        return remote(psend.at[to], pout_ref.at[me], qs_sem.at[r], qr_sem.at[r], to, plane)
+
     def service(step, chunk):
         for slot in ORDER[step]:
             z_wait(slot, chunk)
@@ -205,6 +236,8 @@
             z_last(chunk).start()
         for slot in ORDER[step]:
             f_copy(slot, chunk).start()
+        for r in range(*SPREAD[4 * step - 4 + chunk]):
+            p_copy(r).start()
 
     def transpose_into(source, offset):
         for j in range(half // 128):
@@ -212,24 +245,10 @@
                 :, j * 128 : (j + 1) * 128
             ].T
 
-    def place_of(owner, split):
-        writers = writer_ref[pl.ds(owner, 1), :]
-        mine = lax.broadcasted_iota(jnp.int32, (DP, rows), 0) == writers
-        below = lax.broadcasted_iota(jnp.int32, (rows, rows), 0) < lax.broadcasted_iota(jnp.int32, (rows, rows), 1)
-        before = jnp.dot(
-            mine.astype(jnp.bfloat16), below.astype(jnp.bfloat16), preferred_element_type=jnp.float32
-        )
-        rank = jnp.sum(jnp.where(mine, before, 0.0), axis=0, keepdims=True).astype(jnp.int32)
-        if split:
-            return (rank >> 4) * (DP * 16) + writers * 16 + (rank & 15)
-        return writers * 32 + rank
-
     def onehot(place, start, count):
         slot = start + lax.broadcasted_iota(jnp.int32, (count, rows), 0)
         return (slot == place).astype(jnp.bfloat16)
 
-    loads[0].wait()
-    transpose_into(act_own, core * tokens)
     for load in loads[2:]:
         load.wait()
     e_one = exponent_of(one_in[...])
@@ -239,41 +258,33 @@
     for k, code in enumerate((code_one, code_two)):
         codes[:, (2 * k) * 256 : (2 * k + 1) * 256] = (code >> 8).astype(jnp.float32).astype(jnp.bfloat16)
         codes[:, (2 * k + 1) * 256 : (2 * k + 2) * 256] = (code & 255).astype(jnp.float32).astype(jnp.bfloat16)
-    rest = m_in[...]
-    for k in range(3):
-        piece = rest.astype(jnp.bfloat16)
-        codes[:, (4 + k) * 256 : (5 + k) * 256] = piece
-        rest = rest - piece.astype(jnp.float32)
-    place_m = place_of(me, False)
+    place_code = jnp.round(within_period(m_in[...]) * (1.0 / STEP)).astype(jnp.int32) & 0xFFFFF
+    for k, code in enumerate((place_code >> 12, (place_code >> 4) & 255, place_code & 15)):
+        codes[:, (4 + k) * 256 : (5 + k) * 256] = code.astype(jnp.float32).astype(jnp.bfloat16)
     tile = 256
-    scale_rows = jnp.concatenate([e_one.astype(jnp.int32)] * 4 + [e_two.astype(jnp.int32)] * 4, axis=0)
+    scales = ((e_one.astype(jnp.int32) + OFFSET) << 24) | ((e_two.astype(jnp.int32) + OFFSET) << 16)
     for j in range(1024 // tile):
         packed = jnp.dot(onehot(place_m, j * tile, tile), codes[...], preferred_element_type=jnp.float32)
         q = [packed[:, k * 256 : (k + 1) * 256] for k in range(7)]
-        msend[j * 8 : (j + 1) * 8] = (q[4] + q[5] + q[6]).reshape(8, 32, 256)
+        here = pl.ds(j * 8, 8)
         word = join((q[0] * 256.0 + q[1]).astype(jnp.int32), (q[2] * 256.0 + q[3]).astype(jnp.int32))
-        psend[j * 8 : (j + 1) * 8, 0:32] = word.reshape(8, 32, 256)
-        psend[j * 8 : (j + 1) * 8, 32:40] = jnp.broadcast_to(scale_rows[None], (8, 8, 256))
-
-    def m_copy(r):
-        to = lax.rem(me + r, DP)
-        return remote(msend.at[to], mout_ref.at[me], ms_sem.at[r], mr_sem.at[r], to, plane)
-
-    def p_copy(r):
-        to = lax.rem(me + r, DP)
-        return remote(psend.at[to], pout_ref.at[me], qs_sem.at[r], qr_sem.at[r], to, plane)
-
-    def m_start(r, carry):
-        m_copy(r).start()
+        psend[here, 0:32] = word.reshape(8, 32, 256)
+        high = (q[4] * 256.0 + q[5]).astype(jnp.int32).reshape(8, 32, 256)
+        psend[here, 32:48] = join(high[:, 0:16], high[:, 16:32])
+        low = q[6].astype(jnp.int32).reshape(8, 4, 8, 256)
+        low = low[:, 0] | (low[:, 1] << 4) | (low[:, 2] << 8) | (low[:, 3] << 12)
+        psend[here, 48:56] = low | scales[None]
+
+    def p_start(r, carry):
+        p_copy(r).start()
         return carry
 
-    lax.fori_loop(1, DP, m_start, 0)
-    m_self = pltpu.make_async_copy(msend.at[me], mout_ref.at[me], local_sem.at[5])
     p_self = pltpu.make_async_copy(psend.at[me], pout_ref.at[me], local_sem.at[6])
-    m_self.start()
     p_self.start()
 
     service(1, 0)
+    loads[0].wait()
+    transpose_into(act_own, core * tokens)
     act_copy.wait_recv()
     transpose_into(act_sib, (1 - core) * tokens)
 
@@ -389,12 +400,6 @@
     for slot in ORDER[3] + ORDER[4]:
         reduce(slot)
 
-    def p_start(r, carry):
-        p_copy(r).start()
-        return carry
-
-    lax.fori_loop(1, DP, p_start, 0)
-
     whole(0)
 
     @pl.when(across != 0)
@@ -403,6 +408,7 @@
 
     whole(1)
     p_move(1).start()
+    lax.fori_loop(23, DP, p_start, 0)
 
     owners = [4 * lax.rem(plane + PLANES - shift, PLANES) + 2 * core + along // 2 for shift in shifts]
     for j in range(2):
@@ -431,8 +437,8 @@
                     onehot(place_g, side_of * 512 + i * 256, 256), codes[:, 0:256], preferred_element_type=jnp.float32
                 )
                 q.append((packed[:, 0:128] * 256.0 + packed[:, 128:256]).astype(jnp.int32))
-            gsend[i * 16 : (i + 1) * 16, j, 0:16] = join(q[0], q[1]).reshape(16, 16, 128)
-            gsend[i * 16 : (i + 1) * 16, j, 16:24] = jnp.broadcast_to(exponent[None], (16, 8, 128))
+            gsend[i * 16 : (i + 1) * 16, j * 16 : (j + 1) * 16] = join(q[0], q[1]).reshape(16, 16, 128)
+        gsend[:, 32 + 4 * j : 36 + 4 * j] = jnp.broadcast_to(exponent[None, 0:4], (DP, 4, 128))
 
     def g_copy(r):
         to = lax.rem(me + r, DP)
@@ -471,16 +477,13 @@
         p_move(0).wait_send()
 
     p_move(1).wait_send()
-    m_self.wait()
     p_self.wait()
     g_self.wait()
 
     def finish(r, carry):
         source = lax.rem(me + DP - r, DP)
-        m_copy(r).wait_send()
         p_copy(r).wait_send()
         g_copy(r).wait_send()
-        remote(msend.at[0], mout_ref.at[source], ms_sem.at[r], mr_sem.at[r], source, plane).wait_recv()
         remote(psend.at[0], pout_ref.at[source], qs_sem.at[r], qr_sem.at[r], source, plane).wait_recv()
         remote(gsend.at[0], gout_ref.at[source], gs_sem.at[r], gr_sem.at[r], source, plane).wait_recv()
         return carry
@@ -502,13 +505,12 @@
         main_kernel,
         name="reduce_and_regroup",
         out_shape=(
-            jax.ShapeDtypeStruct((DP, 2, 24, side), i32),
-            jax.ShapeDtypeStruct((DP, 32, width), f32),
-            jax.ShapeDtypeStruct((DP, 40, width), i32),
+            jax.ShapeDtypeStruct((DP, 40, side), i32),
+            jax.ShapeDtypeStruct((DP, 56, width), i32),
             jax.ShapeDtypeStruct((DP + 8, 128), i32),
         ),
         in_specs=[any_space] * 5 + [vmem],
-        out_specs=(any_space, any_space, any_space, vmem),
+        out_specs=(any_space, any_space, vmem),
         scratch_shapes=[
             pltpu.VMEM((tokens, half), bf16),
             pltpu.VMEM((tokens, half), bf16),
@@ -523,13 +525,13 @@
             pltpu.VMEM((2, SIDE - 1) + coded, i32),
             pltpu.VMEM((2,) + coded, i32),
             pltpu.VMEM((2,) + coded, i32),
-            pltpu.VMEM((DP, 2, 24, side), i32),
+            pltpu.VMEM((DP, 40, side), i32),
             pltpu.VMEM((rows, width), f32),
             pltpu.VMEM((rows, width), f32),
             pltpu.VMEM((rows, width), f32),
-            pltpu.VMEM((DP, 32, width), f32),
-            pltpu.VMEM((DP, 40, width), i32),
+            pltpu.VMEM((DP, 56, width), i32),
             pltpu.VMEM((rows, 7 * width), bf16),
+            pltpu.VMEM((DP, rows), i32),
             dma((8,)),
             dma((2,)),
             dma((1,)),
@@ -549,8 +551,6 @@
             dma((DP,)),
             dma((DP,)),
             dma((DP,)),
-            dma((DP,)),
-            dma((DP,)),
         ],
         compiler_params=pltpu.CompilerParams(
             collective_id=0, has_side_effects=True, vmem_limit_bytes=56 * 1024 * 1024
@@ -571,55 +571,98 @@
 
 
 def finish_kernel(
-    base_ref, gradient_hbm, master_hbm, moments_hbm, previous_hbm,
-    delta_ref, high_ref, first_ref, second_ref,
-    gradient_ref, master_ref, moments_ref, previous_ref, rows_ref, sem,
+    base_ref, gradient_hbm, moments_hbm, previous_hbm,
+    delta_hbm, high_hbm, first_hbm, second_hbm,
+    gradient_ref, moments_ref, previous_ref, rows_ref, delta_ref, high_ref, first_ref, second_ref, sem,
 ):
-    loads = [
-        pltpu.make_async_copy(moments_hbm, moments_ref, sem.at[0]),
-        pltpu.make_async_copy(master_hbm, master_ref, sem.at[1]),
-        pltpu.make_async_copy(gradient_hbm, gradient_ref, sem.at[2]),
-        pltpu.make_async_copy(previous_hbm, previous_ref, sem.at[3]),
-    ]
-    for load in loads:
-        load.start()
+    groups = sem.shape[1]
+    count = DP // groups
+    capacity, width = previous_ref.shape
+    block_rows = capacity // groups
+
+    def group_loads(i):
+        some = pl.ds(i * count, count)
+        here = pl.ds(i * block_rows, block_rows)
+        return [
+            pltpu.make_async_copy(moments_hbm.at[some], moments_ref.at[some], sem.at[0, i]),
+            pltpu.make_async_copy(previous_hbm.at[here], previous_ref.at[here], sem.at[2, i]),
+        ]
+
+    def group_stores(i):
+        here = pl.ds(i * block_rows, block_rows)
+        pairs = ((delta_ref, delta_hbm), (high_ref, high_hbm), (first_ref, first_hbm), (second_ref, second_hbm))
+        return [
+            pltpu.make_async_copy(ref.at[here], hbm.at[here], sem.at[3 + k, i]) for k, (ref, hbm) in enumerate(pairs)
+        ]
+
+    gradient_load = pltpu.make_async_copy(gradient_hbm, gradient_ref, sem.at[7, 0])
+    gradient_load.start()
+    for i in range(groups):
+        for load in group_loads(i)[:1]:
+            load.start()
+    for i in range(groups):
+        group_loads(i)[1].start()
     plane = lax.axis_index("tensor")
-    capacity, width = previous_ref.shape
     pair = capacity // DP
-    window = pair + 8
-    row = lax.broadcasted_iota(jnp.int32, (window, 3 * width), 0)
-    for load in loads[:3]:
-        load.wait()
+    row = lax.broadcasted_iota(jnp.int32, (8, 3 * width), 0)
+    gradient_load.wait()
     for owner in range(DP):
+        if owner % count == 0:
+            for load in group_loads(owner // count)[:1]:
+                load.wait()
         parts = []
         for part in range(2):
             source, late = source_of(owner, part, plane)
-            unit = unit_of(gradient_ref[source, late, 16:17, :].astype(jnp.float32))
-            word = gradient_ref[source, late, 0:16, :]
-            parts.append(jnp.concatenate([high_of(word), low_of(word)], axis=0).astype(jnp.float32) * unit)
+            start = pl.multiple_of(late * 16, 8)
+            exponent = gradient_ref[source, 32:40, :]
+            exponent = jnp.where(late == 0, exponent[0:1], exponent[4:5])
+            word = gradient_ref[source, pl.ds(start, 16), :]
+            code = jnp.concatenate([high_of(word), low_of(word)], axis=0).astype(jnp.float32)
+            parts.append(code * unit_of(exponent.astype(jnp.float32)))
         gradient = jnp.concatenate(parts, axis=1)
         word = moments_ref[owner, 0:32, :]
-        one = high_of(word).astype(jnp.float32) * unit_of(moments_ref[owner, 32:33, :].astype(jnp.float32))
-        two = low_of(word).astype(jnp.float32) * unit_of(moments_ref[owner, 36:37, :].astype(jnp.float32))
-        block = jnp.concatenate(adam_rows(gradient, master_ref[owner], one, two), axis=1)
+        tail = moments_ref[owner, 48:56, :]
+        unit_one = unit_of((((tail[0:1] >> 24) & 255) - OFFSET).astype(jnp.float32))
+        unit_two = unit_of((((tail[0:1] >> 16) & 255) - OFFSET).astype(jnp.float32))
+        one = high_of(word).astype(jnp.float32) * unit_one
+        two = low_of(word).astype(jnp.float32) * unit_two
+        first, second = moments_of(gradient, one, two)
+        word = moments_ref[owner, 32:48, :]
+        low = jnp.concatenate([(tail >> (4 * t)) & 15 for t in range(4)], axis=0)
+        code = (jnp.concatenate([(word >> 16) & 0xFFFF, word & 0xFFFF], axis=0) << 4) | low
+        block = jnp.concatenate([code.astype(jnp.float32), first, second], axis=1)
         start = base_ref[owner, 0]
         offset = lax.rem(start, 8)
         aligned = pl.multiple_of(start - offset, 8)
-        block = pltpu.roll(jnp.concatenate([block, block[0:8]], axis=0), offset, 0)
-        target = rows_ref.at[pl.ds(aligned, window), :]
-        target[...] = jnp.where(row >= offset, block, target[...])
-    loads[3].wait()
-    filled = lax.broadcasted_iota(jnp.int32, (capacity, width), 0) < base_ref[DP, 0]
-    delta = jnp.where(filled, (rows_ref[0:capacity, 0:width] - previous_ref[...]) / learn_rate, 0.0)
-    delta_ref[...] = delta
-    high_ref[...] = delta.astype(jnp.bfloat16)
-    first_ref[...] = jnp.where(filled, rows_ref[0:capacity, width : 2 * width], 0.0)
-    second_ref[...] = jnp.where(filled, rows_ref[0:capacity, 2 * width : 3 * width], 0.0)
-
-
-def finish_call(base, gradient, master, moments, previous):
+        block = pltpu.roll(block, offset, 0)
+        head = rows_ref.at[pl.ds(aligned, 8), :]
+        head[...] = jnp.where(row >= offset, block[0:8], head[...])
+        rows_ref[pl.ds(pl.multiple_of(aligned + 8, 8), pair - 8), :] = block[8:pair]
+        rows_ref[pl.ds(pl.multiple_of(aligned + pair, 8), 8), :] = block[0:8]
+    total = base_ref[DP, 0]
+    for i in range(groups):
+        group_loads(i)[1].wait()
+        here = pl.ds(i * block_rows, block_rows)
+        filled = i * block_rows + lax.broadcasted_iota(jnp.int32, (block_rows, width), 0) < total
+        first = rows_ref[here, width : 2 * width]
+        second = rows_ref[here, 2 * width : 3 * width]
+        previous = previous_ref[here, :]
+        ahead = rows_ref[here, 0:width] * STEP - within_period(previous)
+        ahead = ahead - PERIOD * jnp.round(ahead * (1.0 / PERIOD))
+        delta = jnp.where(filled, ahead / learn_rate - step_of(first, second, previous + ahead), 0.0)
+        delta_ref[here, :] = delta
+        high_ref[here, :] = delta.astype(jnp.bfloat16)
+        first_ref[here, :] = jnp.where(filled, first, 0.0)
+        second_ref[here, :] = jnp.where(filled, second, 0.0)
+        for store in group_stores(i):
+            store.start()
+    for i in range(groups):
+        for store in group_stores(i):
+            store.wait()
+
+
+def finish_call(base, gradient, moments, previous):
     capacity, width = previous.shape
-    vmem = pl.BlockSpec(memory_space=pltpu.VMEM)
     any_space = pl.BlockSpec(memory_space=pl.ANY)
     return pl.pallas_call(
         finish_kernel,
@@ -630,24 +673,27 @@
             jax.ShapeDtypeStruct((capacity, width), jnp.float32),
             jax.ShapeDtypeStruct((capacity, width), jnp.float32),
         ),
-        in_specs=[pl.BlockSpec(memory_space=pltpu.SMEM)] + [any_space] * 4,
-        out_specs=(vmem, vmem, vmem, vmem),
+        in_specs=[pl.BlockSpec(memory_space=pltpu.SMEM)] + [any_space] * 3,
+        out_specs=(any_space,) * 4,
         scratch_shapes=[
             pltpu.VMEM(gradient.shape, gradient.dtype),
-            pltpu.VMEM(master.shape, master.dtype),
             pltpu.VMEM(moments.shape, moments.dtype),
             pltpu.VMEM(previous.shape, previous.dtype),
             pltpu.VMEM((capacity + capacity // DP + 8, 3 * width), jnp.float32),
-            pltpu.SemaphoreType.DMA((4,)),
+            pltpu.VMEM((capacity, width), jnp.float32),
+            pltpu.VMEM((capacity, width), jnp.bfloat16),
+            pltpu.VMEM((capacity, width), jnp.float32),
+            pltpu.VMEM((capacity, width), jnp.float32),
+            pltpu.SemaphoreType.DMA((8, 4)),
         ],
         compiler_params=pltpu.CompilerParams(vmem_limit_bytes=60 * 1024 * 1024),
-    )(base, gradient, master, moments, previous)
+    )(base, gradient, moments, previous)
 
 
 def local(activations, cotangent, master, moment_one, moment_two, writer_of, previous):
-    writers = writer_of.reshape(DP, master.shape[0])
-    gradient, masters, moments, base = main_call(activations, cotangent, master, moment_one, moment_two, writers)
-    return finish_call(base, gradient, masters, moments, previous)
+    writers = writer_of.reshape(-1, 128)
+    gradient, moments, base = main_call(activations, cotangent, master, moment_one, moment_two, writers)
+    return finish_call(base, gradient, moments, previous)
 
 
 def solution(mesh):

time: 110 us -> 99.4 us (0.904)
  the two profiles are of different devices: /device:TPU:57 before, /device:TPU:25 now
where the time goes in v4:
time: 99.4 us; the launch traced here: 99.2 us
  Pallas kernels  98.4 us (99%)
    pallas_call x1, Pallas kernels, main_call(): pl.pallas_call(main_kernel, name='reduce_and_regroup', out_shape=(jax.Sha...  92.1 us
    pallas_call x1, Pallas kernels, finish_call(): pl.pallas_call(finish_kernel, name='update_and_place', out_shape=(jax.Sha...  6.23 us

profile of v4, /device:TPU:25, one launch (start us, length us, event | category | flops | bytes accessed | tf_op | source)
XLA Modules:
  0.0 99.2 jit_solution(15054249975051519724)
XLA Ops:
  0.6 92.1 %reduce_and_regroup.1 = (s32[32,40,128]{2,1,0:T(8,128)}, s32[32,56,256]{2,1,0:T(8,128)}, s32[40,128]{1,0:T(8,128)}) custom-call(bf16[768,2048]{1,0:T(8,128)(2,1)} %act_ref.1, bf16[768,256]{1,0:T(8,128)(2,1)} %cot_ref.1, f32[512,256]{1,0:T(8,128)} %master_ref.1, f32[512,256]{1,0:T(8,128)} %one_ref.1, f32[512,256]{1,0:T(8,128)} %two_ref.1, s32[128,128]{1,0:T(8,128)} %bitcast.1), custom_call_target="tpu_custom_call" | custom-call | flops 6442450944 | bytes 8388608 | tf_op jit(solution)/shard_map/reduce_and_regroup/pallas_call | solution.py:504
  92.8 6.2 %update_and_place.1 = (f32[1024,256]{1,0:T(8,128)}, bf16[1024,256]{1,0:T(8,128)(2,1)}, f32[1024,256]{1,0:T(8,128)}, f32[1024,256]{1,0:T(8,128)}) custom-call(s32[40,128]{1,0:T(8,128)} %get-tuple-element.7.base_ref, s32[32,40,128]{2,1,0:T(8,128)} %get-tuple-element.8.gradient_hbm, s32[32,56,256]{2,1,0:T(8,128)} %get-tuple-element.9.moments_hbm, ...), custom_call_target="tpu_custom_call" | custom-call | tf_op jit(solution)/shard_map/update_and_place/pallas_call | solution.py:667

commit v5 on v4

--- a/solution.py
+++ b/solution.py
@@ -26,7 +26,7 @@
 PERIOD = 0.625
 STEP = PERIOD / 2**20
 OFFSET = 128
-SPREAD = ((1, 4), (4, 7), (7, 10), (10, 13), (13, 15), (15, 17), (17, 19), (19, 21), (21, 22), (22, 23), (23, 23), (23, 23), (23, 23), (23, 23), (23, 23), (23, 23))
+SPREAD = ((1, 6), (6, 11), (11, 15), (15, 19), (19, 21), (21, 23), (23, 23), (23, 23), (23, 23), (23, 23), (23, 23), (23, 23), (23, 23), (23, 23), (23, 23), (23, 23))
 ORDER = ((0,), (1, 7), (2, 6), (3, 5), (4,))
 
 

time: 99.4 us -> 96.3 us (0.969)
  the two profiles are of different devices: /device:TPU:25 before, /device:TPU:57 now
where the time goes in v5:
time: 96.3 us; the launch traced here: 95.9 us
  Pallas kernels  95.1 us (99%)
    pallas_call x1, Pallas kernels, main_call(): pl.pallas_call(main_kernel, name='reduce_and_regroup', out_shape=(jax.Sha...  88.8 us
    pallas_call x1, Pallas kernels, finish_call(): pl.pallas_call(finish_kernel, name='update_and_place', out_shape=(jax.Sha...  6.23 us

profile of v5, /device:TPU:57, one launch (start us, length us, event | category | flops | bytes accessed | tf_op | source)
XLA Modules:
  0.0 95.9 jit_solution(13858826285326819669)
XLA Ops:
  0.6 88.8 %reduce_and_regroup.1 = (s32[32,40,128]{2,1,0:T(8,128)}, s32[32,56,256]{2,1,0:T(8,128)}, s32[40,128]{1,0:T(8,128)}) custom-call(bf16[768,2048]{1,0:T(8,128)(2,1)} %act_ref.1, bf16[768,256]{1,0:T(8,128)(2,1)} %cot_ref.1, f32[512,256]{1,0:T(8,128)} %master_ref.1, f32[512,256]{1,0:T(8,128)} %one_ref.1, f32[512,256]{1,0:T(8,128)} %two_ref.1, s32[128,128]{1,0:T(8,128)} %bitcast.1), custom_call_target="tpu_custom_call" | custom-call | flops 6442450944 | bytes 8388608 | tf_op jit(solution)/shard_map/reduce_and_regroup/pallas_call | solution.py:504
  89.5 6.2 %update_and_place.1 = (f32[1024,256]{1,0:T(8,128)}, bf16[1024,256]{1,0:T(8,128)(2,1)}, f32[1024,256]{1,0:T(8,128)}, f32[1024,256]{1,0:T(8,128)}) custom-call(s32[40,128]{1,0:T(8,128)} %get-tuple-element.7.base_ref, s32[32,40,128]{2,1,0:T(8,128)} %get-tuple-element.8.gradient_hbm, s32[32,56,256]{2,1,0:T(8,128)} %get-tuple-element.9.moments_hbm, ...), custom_call_target="tpu_custom_call" | custom-call | tf_op jit(solution)/shard_map/update_and_place/pallas_call | solution.py:667

commit v6 on v5

--- a/solution.py
+++ b/solution.py
@@ -485,10 +485,15 @@
         p_copy(r).wait_send()
         g_copy(r).wait_send()
         remote(psend.at[0], pout_ref.at[source], qs_sem.at[r], qr_sem.at[r], source, plane).wait_recv()
+        return carry
+
+    def arrive(r, carry):
+        source = lax.rem(me + DP - r, DP)
         remote(gsend.at[0], gout_ref.at[source], gs_sem.at[r], gr_sem.at[r], source, plane).wait_recv()
         return carry
 
     lax.fori_loop(1, DP, finish, 0)
+    lax.fori_loop(1, DP, arrive, 0)
 
 
 def main_call(activations, cotangent, master, moment_one, moment_two, writers):

time: 96.3 us -> 96.2 us (level)
  no operation moved by 1% of the time
where the time goes in v6:
time: 96.2 us; the launch traced here: 95.8 us
  Pallas kernels  95 us (99%)
    pallas_call x1, Pallas kernels, main_call(): pl.pallas_call(main_kernel, name='reduce_and_regroup', out_shape=(jax.Sha...  88.8 us
    pallas_call x1, Pallas kernels, finish_call(): pl.pallas_call(finish_kernel, name='update_and_place', out_shape=(jax.Sha...  6.23 us

profile of v6, /device:TPU:57, one launch (start us, length us, event | category | flops | bytes accessed | tf_op | source)
XLA Modules:
  0.0 95.8 jit_solution(13489528825212580106)
XLA Ops:
  0.6 88.8 %reduce_and_regroup.1 = (s32[32,40,128]{2,1,0:T(8,128)}, s32[32,56,256]{2,1,0:T(8,128)}, s32[40,128]{1,0:T(8,128)}) custom-call(bf16[768,2048]{1,0:T(8,128)(2,1)} %act_ref.1, bf16[768,256]{1,0:T(8,128)(2,1)} %cot_ref.1, f32[512,256]{1,0:T(8,128)} %master_ref.1, f32[512,256]{1,0:T(8,128)} %one_ref.1, f32[512,256]{1,0:T(8,128)} %two_ref.1, s32[128,128]{1,0:T(8,128)} %bitcast.1), custom_call_target="tpu_custom_call" | custom-call | flops 6442450944 | bytes 8388608 | tf_op jit(solution)/shard_map/reduce_and_regroup/pallas_call | solution.py:509
  89.4 6.2 %update_and_place.1 = (f32[1024,256]{1,0:T(8,128)}, bf16[1024,256]{1,0:T(8,128)(2,1)}, f32[1024,256]{1,0:T(8,128)}, f32[1024,256]{1,0:T(8,128)}) custom-call(s32[40,128]{1,0:T(8,128)} %get-tuple-element.7.base_ref, s32[32,40,128]{2,1,0:T(8,128)} %get-tuple-element.8.gradient_hbm, s32[32,56,256]{2,1,0:T(8,128)} %get-tuple-element.9.moments_hbm, ...), custom_call_target="tpu_custom_call" | custom-call | tf_op jit(solution)/shard_map/update_and_place/pallas_call | solution.py:672
